TPU v7x, 32 devices: a whole 2x2x4 slice. The times are simulated.
32 devices in a mesh: pre: 8 (over y, x, core), rsp: 4 (over z).
Axes of the slice: x: 2, y: 2, z: 4, core: 2. Of those that a mesh axis runs over, the one named last changes fastest.
Arguments:
- prompt_query: bfloat16 [1024, 2560], P(('pre', 'rsp')), may hold values from -100 to 100
- prompt_k: bfloat16 [1024, 512], P('pre'), may hold values from -5 to 5
- prompt_value: bfloat16 [1024, 512], P('pre'), may hold values from -6 to 6
- prompt_output: bfloat16 [1024, 2560], P(('pre', 'rsp')), may hold values from -6 to 6
- prompt_output_gradient: bfloat16 [1024, 2560], P(('pre', 'rsp')), may hold values from -24 to 24
- reply_query: bfloat16 [4, 2048, 2560], P('rsp', 'pre'), may hold values from -100 to 100
- reply_key: bfloat16 [4, 2048, 512], P('rsp', 'pre'), may hold values from -6 to 6
- reply_value: bfloat16 [4, 2048, 512], P('rsp', 'pre'), may hold values from -6 to 6
- reply_output: bfloat16 [4, 2048, 2560], P('rsp', 'pre'), may hold values from -6 to 6
- reply_output_gradient: bfloat16 [4, 2048, 2560], P('rsp', 'pre'), may hold values from -24 to 24
- reply_len: int32 [8], replicated, may hold values from 1 to 1024, 5120 in all
- reply_slot: int32 [8], replicated, may hold values from 0 to 7, each once
Outputs:
- prompt_dq: bfloat16 [1024, 2560], P(('pre', 'rsp'))
- prompt_dk: bfloat16 [1024, 512], P(('pre', 'rsp'))
- prompt_dv: bfloat16 [1024, 512], P(('pre', 'rsp'))
- reply_dq: bfloat16 [4, 2048, 2560], P('rsp', 'pre')
- reply_dk: bfloat16 [4, 2048, 512], P('rsp', 'pre')
- reply_dv: bfloat16 [4, 2048, 512], P('rsp', 'pre')
Inputs may be any that keep to these rules, and one draw needn't show every extreme that they name: `reply_len`: one response is exactly 1024 long; the lengths sum to 5120, rounded down. `reply_slot`: every slot is taken by exactly one response.
All inputs are finite; a program needn't handle non-finite values.
Results may differ from a plain program's by a relative error of at most 0.012.
Values may be sent and summed in bfloat16 or wider, within the bound.
No kernel may reach another device: no remote copies, remote signals or barrier semaphores. Data moves between devices by JAX's collectives and lax.ppermute only.
A program may use at most 128 MiB of HBM per device.

v0:
```python
import functools
import math

import jax
import jax.numpy as jnp
from jax import lax
from jax.experimental import pallas as pl
from jax.experimental.pallas import tpu as pltpu
from jax.sharding import PartitionSpec as P

QUERY_HEADS = 20
KEY_VALUE_HEADS = 4
GROUP = QUERY_HEADS // KEY_VALUE_HEADS
HEAD_WIDTH = 128
RESP_DEV = 2
CORES = 2
LOCAL_HEADS = KEY_VALUE_HEADS // CORES
GROUP_WIDTH = GROUP * HEAD_WIDTH

SCALE = HEAD_WIDTH ** (-0.5)
SCALE_LOG2 = SCALE * math.log2(math.e)
PART = 128
NEGATIVE_FLOOR = -1e30
DEAD = 1e30
F32 = jnp.float32
BF16 = jnp.bfloat16
VMEM = pl.BlockSpec(memory_space=pltpu.VMEM)
SMEM = pl.BlockSpec(memory_space=pltpu.SMEM)
HBM = pl.BlockSpec(memory_space=pltpu.HBM)


VMEM_MIB = 40
SMALL_MIB = 24
LARGE_MIB = 58


def params(mib):
    return pltpu.CompilerParams(vmem_limit_bytes=mib * 1024 * 1024)


def dot(a, b, over=(1, 0)):
    return lax.dot_general(
        a, b, (((over[0],), (over[1],)), ((), ())), preferred_element_type=F32
    )


def iota(shape, axis):
    return lax.broadcasted_iota(jnp.int32, shape, axis)


def sorting(rows):
    half = rows // RESP_DEV
    out = iota((rows, rows), 0)
    source = jnp.where(out < half, RESP_DEV * out, RESP_DEV * (out - half) + 1)
    return (iota((rows, rows), 1) == source).astype(BF16)


def unsorting(rows):
    half = rows // RESP_DEV
    out = iota((rows, rows), 1)
    source = jnp.where(out < half, RESP_DEV * out, RESP_DEV * (out - half) + 1)
    return (iota((rows, rows), 0) == source).astype(BF16)


def lanes(index, width):
    return pl.ds(pl.multiple_of(index * width, width), width)


def head_of(core, cross, local):
    owner = (1 - core) if cross else core
    return owner * LOCAL_HEADS + local


def fetch(pairs, sems):
    copies = [pltpu.make_async_copy(src, dst, sems.at[i]) for i, (src, dst) in enumerate(pairs)]
    for copy in copies:
        copy.start()
    return copies


def prepare_keys(pk, pv, rk, rv, mine0, theirs0, mine1, theirs, token, *scratch):
    core = lax.rem(lax.axis_index("pre"), CORES)
    bufs, sems = scratch[:-1], scratch[-1]
    copies = fetch(zip((pk, pv, rk, rv), bufs), sems)
    prompt = pk.shape[0]
    order = sorting(rk.shape[0])
    for copy in copies:
        copy.wait()
    pk, pv, rk, rv = bufs
    for local, outs in enumerate(((mine0, theirs.at[0]), (mine1, theirs.at[1]))):
        for cross, out in enumerate(outs):
            span = lanes(head_of(core, cross, local), HEAD_WIDTH)
            for part, (p, r) in enumerate(((pk, rk), (pv, rv))):
                to = slice(part * HEAD_WIDTH, (part + 1) * HEAD_WIDTH)
                out[:prompt, to] = p[:, span]
                out[prompt:, to] = dot(order, r[:, span]).astype(BF16)
    theirs0[...] = theirs[0]
    token[...] = jnp.zeros_like(token)


def prepare_rows(place, token, pq, po, pg, rq, ro, rg, *refs):
    (theirs, *mine), bufs, sems = refs[: 1 + LOCAL_HEADS], refs[1 + LOCAL_HEADS : -1], refs[-1]
    outs = [out for local in range(LOCAL_HEADS) for out in (theirs.at[local], mine[local])]
    core = place[1]
    reply = rq.shape[0]
    sources = (pq, po, pg, rq, ro, rg)
    pairs = []
    for step in range(KEY_VALUE_HEADS):
        span = lanes(head_of(core, 1 - step % CORES, step // CORES), GROUP_WIDTH)
        pairs += [(source.at[:, span], buf.at[step]) for source, buf in zip(sources, bufs)]
    copies = fetch(pairs, sems)
    order = sorting(reply)
    column = iota((GROUP_WIDTH, HEAD_WIDTH), 1)
    pick = (column // 3 == iota((GROUP_WIDTH, HEAD_WIDTH), 0) // HEAD_WIDTH).astype(BF16)

    def delta(gradient, output):
        product = gradient.astype(F32) * output.astype(F32)
        high = product.astype(BF16)
        low = (product - high.astype(F32)).astype(BF16)
        value = dot(high, pick) + dot(low, pick)
        first = value.astype(BF16).astype(F32)
        second = (value - first).astype(BF16).astype(F32)
        part = iota(value.shape, 1) % 3
        return jnp.where(part == 0, first, jnp.where(part == 1, second, value - first - second)).astype(BF16)

    for step, out in enumerate(outs):
        for copy in copies[step * len(sources) : (step + 1) * len(sources)]:
            copy.wait()
        pq, po, pg, rq, ro, rg = (buf[step] for buf in bufs)
        out[reply:, :GROUP_WIDTH] = pq
        out[reply:, GROUP_WIDTH : 2 * GROUP_WIDTH] = pg
        out[reply:, 2 * GROUP_WIDTH :] = delta(pg, po)
        out[:reply, :GROUP_WIDTH] = dot(order, rq).astype(BF16)
        gradient = dot(order, rg).astype(BF16)
        out[:reply, GROUP_WIDTH : 2 * GROUP_WIDTH] = gradient
        out[:reply, 2 * GROUP_WIDTH :] = delta(gradient, dot(order, ro).astype(BF16))


def attend(sizes, joint_keys, place, reply_len, reply_slot, *refs):
    chips, reply_own, prompt_own, prompt_rows, prompt_keys = sizes
    own_positions = reply_own // RESP_DEV
    positions = CORES * own_positions
    chip_prompt = CORES * prompt_keys
    block = 2 * positions
    prompt_blocks = chips * chip_prompt // block
    rows_in, refs = (refs[0], refs[1].at[int(joint_keys)]), refs[2:]
    count = chips if joint_keys else chips * CORES
    keys_in, refs = refs[:count], refs[count:]
    query_out, refs = refs[:2], refs[2:]
    keys_out, refs = refs[:chips], refs[chips:]
    prompt_out, refs = (refs[:chips], refs[chips:]) if joint_keys else (keys_out, refs)
    keys, keys_t, total, query, gradient, query_t, gradient_t, deltas, delta, scores, peaks, top, mass, *refs = refs
    query_grad, stages = refs[0], (refs[1:3], refs[3:5])
    chip, core, group = place[0], place[1], place[2]

    pick = (iota((8, HEAD_WIDTH), 1) // 3 == iota((8, HEAD_WIDTH), 0)).astype(BF16)
    for other in range(CORES):
        deltas[other] = dot(pick, rows_in[other][:, 2 * GROUP_WIDTH :], (1, 1))

    for index in range(chips * CORES):
        away, other = index // CORES, index % CORES
        source = keys_in[away].at[other] if joint_keys else keys_in[index]
        source = source if len(source.shape) == 2 else source.at[0]
        at = away * chip_prompt + other * prompt_keys
        keys[at : at + prompt_keys] = source[:prompt_keys]
        for slot in range(RESP_DEV):
            at = chips * chip_prompt + (slot * chips + away) * positions + other * own_positions
            begin = prompt_keys + slot * own_positions
            keys[at : at + own_positions] = source[begin : begin + own_positions]
    total[...] = jnp.zeros_like(total)

    unit = (iota((HEAD_WIDTH, HEAD_WIDTH), 0) == iota((HEAD_WIDTH, HEAD_WIDTH), 1)).astype(BF16)

    def transpose_block(index, carry):
        rows = pl.ds(pl.multiple_of(index * block, block), block)
        keys_t[index] = dot(unit, keys[rows, :HEAD_WIDTH], (1, 1)).astype(BF16)
        return carry

    lax.fori_loop(0, keys_t.shape[0], transpose_block, 0)

    def score_block(region, place_in, width, chunks, hidden, count=block):
        rows = pl.ds(pl.multiple_of(region * block, block), count)
        key_rows = keys[rows, :HEAD_WIDTH]
        for chunk in range(chunks):
            span = slice(chunk * width, (chunk + 1) * width)
            value = dot(key_rows, query_t[:, span]) * SCALE_LOG2
            if hidden is not None:
                value = jnp.where(hidden, NEGATIVE_FLOOR, value)
            split = value.reshape(count // 8, 8, width)
            peak, summed = top[:, span], mass[:, span]
            for part in range(count // PART):
                piece = split[part * PART // 8 : (part + 1) * PART // 8]
                now = jnp.maximum(peak, jnp.max(piece, axis=0))
                shifted = jnp.exp2(piece - now[None])
                scores[place_in, part * PART : (part + 1) * PART, span] = shifted.reshape(PART, width)
                peaks[place_in, part, :, span] = now
                summed = summed * jnp.exp2(peak - now) + jnp.sum(shifted, axis=0)
                peak = now
            top[:, span], mass[:, span] = peak, summed

    def weigh(region, place_in, width, chunks, log_mass, stage, count=block, earlier=None):
        rows = pl.ds(pl.multiple_of(region * block, block), count)
        value_rows = keys[rows, HEAD_WIDTH:]
        for chunk in range(chunks):
            span = slice(chunk * width, (chunk + 1) * width)
            dp = dot(value_rows, gradient_t[:, span])
            for part in range(count // PART):
                at = slice(part * PART, (part + 1) * PART)
                factor = jnp.exp2(peaks[place_in, part, :, span] - log_mass[chunk])
                p = scores[place_in, at, span].reshape(PART // 8, 8, width) * factor[None]
                p = p.reshape(PART, width)
                stage[0][at, span] = p.astype(BF16)
                stage[1][at, span] = (p * (dp[at] - delta[0:1, span])).astype(BF16)
            if earlier is not None:
                multiply(*earlier, width, chunks, chunk)
        if earlier is not None:
            for chunk in range(chunks, 3):
                multiply(*earlier, width, chunks, chunk)

    def multiply(region, stage, count, width, chunks, part):
        rows = pl.ds(pl.multiple_of(region * block, block), count)
        used = width * chunks
        if part == 0:
            total[rows, HEAD_WIDTH:] += dot(stage[0][:count, :used], gradient[:used])
        elif part == 1:
            total[rows, :HEAD_WIDTH] += dot(stage[1][:count, :used], query[:used])
        elif part == 2:
            query_grad[:, :used] += dot(keys_t[region, :, :count], stage[1][:count, :used])

    def grad_blocks(blocks, region_of, width, chunks, log_mass, begin_with):
        first, second = stages

        def later(index, stage, earlier_stage):
            earlier = region_of(index - 1), earlier_stage, block
            weigh(region_of(index), index, width, chunks, log_mass, stage, earlier=earlier)

        def last(stage):
            for part in range(3):
                multiply(region_of(blocks - 1), stage, block, width, chunks, part)

        begin_with(first, second)

        def two(index, carry):
            later(2 * index + 1, first, second)

            @pl.when(2 * index + 2 < blocks)
            def _():
                later(2 * index + 2, second, first)

            return carry

        lax.fori_loop(0, blocks // 2, two, 0)

        @pl.when(blocks % 2 == 0)
        def _():
            last(first)

        @pl.when(blocks % 2 == 1)
        def _():
            last(second)

    def turn(all_rows):
        query_t[:, :all_rows] = dot(unit, query[:all_rows], (1, 1)).astype(BF16)
        gradient_t[:, :all_rows] = dot(unit, gradient[:all_rows], (1, 1)).astype(BF16)

    def begin(all_rows):
        top[:, :all_rows] = jnp.full((8, all_rows), NEGATIVE_FLOOR, F32)
        mass[:, :all_rows] = jnp.zeros((8, all_rows), F32)
        query_grad[:, :all_rows] = jnp.zeros((HEAD_WIDTH, all_rows), F32)

    def log_masses(width, chunks, live):
        found = []
        for chunk in range(chunks):
            span = slice(chunk * width, (chunk + 1) * width)
            peak = jnp.max(top[:, span], axis=0, keepdims=True)
            summed = jnp.sum(mass[:, span] * jnp.exp2(top[:, span] - peak), axis=0, keepdims=True)
            found.append(jnp.where(live, peak + jnp.log2(summed), DEAD))
        return found

    def absolute(index, half):
        return index + jnp.where(index < half, core * half, -core * half)

    def reply_tile(slot, carry):
        length = jnp.int32(0)
        for response in range(reply_len.shape[0]):
            mine = reply_slot[response] == group * RESP_DEV + slot
            length = length + jnp.where(mine, reply_len[response], 0)
        first = chip * positions
        source = pl.ds(pl.multiple_of(slot * own_positions, own_positions), own_positions)

        @pl.when(length > first)
        def _():
            for head in range(GROUP):
                for other in range(CORES):
                    at = head * positions + other * own_positions
                    to = slice(at, at + own_positions)
                    left = slice(head * HEAD_WIDTH, (head + 1) * HEAD_WIDTH)
                    right = slice(GROUP_WIDTH + head * HEAD_WIDTH, GROUP_WIDTH + (head + 1) * HEAD_WIDTH)
                    query[to] = rows_in[other][source, left]
                    gradient[to] = rows_in[other][source, right]
                    for which in range(RESP_DEV):
                        @pl.when(slot == which)
                        def _():
                            delta[0:1, to] = deltas[
                                other, head : head + 1, which * own_positions : (which + 1) * own_positions
                            ]
            begin(GROUP * positions)
            turn(GROUP * positions)
            base = prompt_blocks + slot * (chips // 2)
            past = prompt_blocks + chip // 2

            def region_of(index):
                reply = base + ((index - prompt_blocks) ^ (chip // 2))
                return jnp.where(index < prompt_blocks, index, reply)

            def stats(index, carry):
                score_block(region_of(index), index, positions, GROUP, None)
                return carry

            lax.fori_loop(0, past, stats, 0)
            row_at = absolute(iota((1, positions), 1), own_positions)
            odd = chip % 2 == 1

            def own_stats(count):
                key = iota((count, 1), 0)
                key_at = jnp.where(key < positions, absolute(key, own_positions), -1)
                score_block(base, past, positions, GROUP, key_at > row_at, count)

            @pl.when(odd)
            def _():
                own_stats(block)

            @pl.when(jnp.logical_not(odd))
            def _():
                own_stats(positions)

            live = first + row_at < length
            log_mass = log_masses(positions, GROUP, live)


            def own_grads(stage, next_stage):
                def run(count):
                    weigh(base, past, positions, GROUP, log_mass, stage, count)
                    earlier = base, stage, count
                    weigh(region_of(0), 0, positions, GROUP, log_mass, next_stage, earlier=earlier)

                @pl.when(odd)
                def _():
                    run(block)

                @pl.when(jnp.logical_not(odd))
                def _():
                    run(positions)

            grad_blocks(past, region_of, positions, GROUP, log_mass, own_grads)
            for head in range(GROUP):
                turned = (query_grad[:, head * positions : (head + 1) * positions].T * SCALE).astype(BF16)
                for other in range(CORES):
                    query_out[other][source, head * HEAD_WIDTH : (head + 1) * HEAD_WIDTH] = turned[
                        other * own_positions : (other + 1) * own_positions
                    ]

        @pl.when(length <= first)
        def _():
            for other in range(CORES):
                query_out[other][source, :] = jnp.zeros((own_positions, GROUP_WIDTH), BF16)

        return carry

    lax.fori_loop(0, RESP_DEV, reply_tile, 0)

    head_rows = CORES * prompt_own
    used = GROUP * head_rows
    all_rows = -(-used // 128) * 128
    if all_rows > used:
        query[used:all_rows] = jnp.zeros((all_rows - used, HEAD_WIDTH), BF16)
        gradient[used:all_rows] = jnp.zeros((all_rows - used, HEAD_WIDTH), BF16)
    delta[0:1, :all_rows] = jnp.zeros((1, all_rows), F32)
    for head in range(GROUP):
        for other in range(CORES):
            at = head * head_rows + other * prompt_own
            to = slice(at, at + prompt_own)
            left = slice(head * HEAD_WIDTH, (head + 1) * HEAD_WIDTH)
            right = slice(GROUP_WIDTH + head * HEAD_WIDTH, GROUP_WIDTH + (head + 1) * HEAD_WIDTH)
            query[to] = rows_in[other][reply_own:, left]
            gradient[to] = rows_in[other][reply_own:, right]
            delta[0:1, to] = deltas[other, head : head + 1, reply_own:]
    begin(all_rows)
    turn(all_rows)
    lane = iota((1, all_rows), 1)
    within = lane
    for head in range(1, GROUP):
        within = within - jnp.where(lane >= head * head_rows, head_rows, 0)
    offset = jnp.where(within < prompt_own, within, within - prompt_own)
    row_core = jnp.where(within < prompt_own, core, 1 - core)
    real = (lane < used) & (offset < prompt_rows)
    row_at = jnp.where(
        real, (chip * CORES + row_core) * prompt_keys + group * prompt_rows + offset, -1
    )
    per_block = max(block // chip_prompt, 1)
    block_parts = max(chip_prompt // block, 1)
    pair = chip // per_block
    seen = (pair + 1) * block_parts

    def prompt_region(index):
        return (index // block_parts ^ pair) * block_parts + index % block_parts

    def prompt_stats(index, carry):
        key = iota((block, 1), 0) + index % block_parts * block
        key_chip = ((index // block_parts ^ pair) * per_block + key // chip_prompt) ^ chip
        key_at = key_chip * chip_prompt + absolute(key % chip_prompt, prompt_keys)
        score_block(prompt_region(index), index, all_rows, 1, key_at > row_at)
        return carry

    lax.fori_loop(0, seen, prompt_stats, 0)
    log_mass = log_masses(all_rows, 1, real)


    def prompt_grads(index, carry):
        weigh(prompt_region(index), index, all_rows, 1, log_mass, stages[0])
        for part in range(3):
            multiply(prompt_region(index), stages[0], block, all_rows, 1, part)
        return carry

    lax.fori_loop(0, seen, prompt_grads, 0)
    turned = (query_grad[:, :all_rows].T * SCALE).astype(BF16)
    for head in range(GROUP):
        for other in range(CORES):
            at = head * head_rows + other * prompt_own
            query_out[other][reply_own:, head * HEAD_WIDTH : (head + 1) * HEAD_WIDTH] = turned[
                at : at + prompt_own
            ]

    def put(out, at, count):
        out[:, :HEAD_WIDTH] = (total[at : at + count, :HEAD_WIDTH] * SCALE).astype(BF16)
        out[:, HEAD_WIDTH:] = total[at : at + count, HEAD_WIDTH:].astype(BF16)

    for index in range(chips * CORES):
        away, other = index // CORES, index % CORES
        put(prompt_out[away].at[other, :prompt_keys], away * chip_prompt + other * prompt_keys, prompt_keys)
        for slot in range(RESP_DEV):
            at = chips * chip_prompt + (slot * chips + away) * positions + other * own_positions
            to = slot * own_positions + (0 if joint_keys else prompt_keys)
            put(keys_out[away].at[other, to : to + own_positions], at, own_positions)


def add(first, *rest):
    value = first.astype(F32)
    for part in rest:
        value = value + part.astype(F32)
    return value


def collect_first(chips, place, *refs):
    parts, prompt_parts, refs = refs[:chips], refs[chips : 2 * chips], refs[2 * chips :]
    mine, theirs, outs, summed = refs[0], refs[1], refs[2:-1], refs[-1]
    groups, rows = len(outs), outs[0].shape[1]
    prompt_keys = groups * rows
    mine[...] = add(*(part[0, prompt_keys:] for part in parts))
    theirs[...] = add(*(part[1, prompt_keys:] for part in parts)).astype(BF16)
    for other in range(CORES):
        summed[other] = add(*(part[other, :prompt_keys] for part in parts))
        summed[CORES + other] = add(*(part[other] for part in prompt_parts))
    for shift in range(groups):
        at = pl.ds(pl.multiple_of(lax.rem(place[2] + shift, groups) * rows, rows), rows)
        for index in range(summed.shape[0]):
            outs[shift][index] = summed[index, at].astype(BF16)


def collect_second(chips, *refs):
    parts, slices, (theirs0, mine, prompt, theirs) = refs[:chips], refs[chips:-4], refs[-4:]
    reply, rows = theirs0.shape[0], prompt.shape[1]
    step = max(rows, 16)
    mine[...] = add(*(part[0] for part in parts))
    theirs[:reply] = theirs0[...]
    theirs[reply : 2 * reply] = add(*(part[1] for part in parts)).astype(BF16)
    for local in range(LOCAL_HEADS):
        prompt[local] = add(*(part[CORES * local] for part in slices))
        at = 2 * reply + local * step
        theirs[at : at + rows] = add(*(part[CORES * local + 1] for part in slices)).astype(BF16)


def finish_queries(place, *refs):
    queries, prompt_dq, reply_dq = refs[:-2], refs[-2], refs[-1]
    reply = reply_dq.shape[0]
    order = unsorting(reply)
    for index, query in enumerate(queries):
        span = lanes(head_of(place[1], index % CORES, index // CORES), GROUP_WIDTH)
        reply_dq[:, span] = dot(order, query[:reply]).astype(BF16)
        prompt_dq[:, span] = query[reply:]


def finish_keys(place, reply0, reply1, prompts, theirs, prompt_dk, prompt_dv, reply_dk, reply_dv):
    reply, rows = reply_dk.shape[0], prompt_dk.shape[0]
    step = max(rows, 16)
    order = unsorting(reply)
    for local in range(LOCAL_HEADS):
        for other in range(CORES):
            span = lanes(head_of(place[1], other, local), HEAD_WIDTH)
            if other:
                value = theirs[local * reply : (local + 1) * reply]
                prompt = theirs[2 * reply + local * step : 2 * reply + local * step + rows]
            else:
                value = (reply1 if local else reply0)[...].astype(BF16)
                prompt = prompts[local].astype(BF16)
            value = dot(order, value).astype(BF16)
            reply_dk[:, span] = value[:, :HEAD_WIDTH]
            reply_dv[:, span] = value[:, HEAD_WIDTH:]
            prompt_dk[:, span] = prompt[:, :HEAD_WIDTH]
            prompt_dv[:, span] = prompt[:, HEAD_WIDTH:]


def on_device(
    prompt_query,
    prompt_k,
    prompt_value,
    prompt_output,
    prompt_output_gradient,
    reply_query,
    reply_key,
    reply_value,
    reply_output,
    reply_output_gradient,
    reply_len,
    reply_slot,
):
    devices = lax.axis_size("pre")
    groups = lax.axis_size("rsp")
    chips = devices // CORES
    prompt_rows = prompt_query.shape[0]
    prompt_own = -(-prompt_rows // 16) * 16
    prompt_keys = prompt_k.shape[0]
    reply_own = reply_query.shape[1]
    own_positions = reply_own // RESP_DEV
    positions = CORES * own_positions
    chip_prompt = CORES * prompt_keys
    block = 2 * positions
    assert (chip_prompt % block == 0 or block % chip_prompt == 0) and chips > 1 and chips & (chips - 1) == 0
    pre_index = lax.axis_index("pre")
    place = jnp.stack([lax.div(pre_index, CORES), lax.rem(pre_index, CORES), lax.axis_index("rsp")])

    def shape(*dims, dtype=BF16):
        return jax.ShapeDtypeStruct(dims, dtype)

    def move(array, away, cross=0):
        pairs = [(p, (p // CORES ^ away) * CORES + (p % CORES ^ cross)) for p in range(devices)]
        return lax.ppermute(array, "pre", pairs)

    def swap(array):
        return move(array, 0, 1)

    def call(kernel, name, mib, inputs, outs, scalars=1, spec=VMEM, **more):
        return pl.pallas_call(
            kernel,
            out_shape=outs,
            in_specs=[SMEM] * scalars + [spec] * (len(inputs) - scalars),
            out_specs=[VMEM] * len(outs),
            compiler_params=params(mib),
            name=name,
            **more,
        )(*inputs)

    relayed = chips == 4
    key_shape = (prompt_keys + reply_own, 2 * HEAD_WIDTH)
    mine0, theirs0, mine1, theirs, token = call(
        prepare_keys,
        "prepare_keys",
        LARGE_MIB,
        (prompt_k, prompt_value, reply_key[0], reply_value[0]),
        [shape(*key_shape)] * 3 + [shape(LOCAL_HEADS, *key_shape), shape(8, 128, dtype=F32)],
        scalars=0,
        spec=HBM,
        scratch_shapes=[
            pltpu.VMEM((rows, KEY_VALUE_HEADS * HEAD_WIDTH), BF16)
            for rows in (prompt_keys, prompt_keys, reply_own, reply_own)
        ]
        + [pltpu.SemaphoreType.DMA((4,))],
    )
    blocks0 = {(0, 0): mine0, (0, 1): swap(theirs)}
    for away in range(1, 3 if relayed else chips):
        blocks0[away, 0] = move(mine0, away)
        blocks0[away, 1] = move(theirs0, away, 1)
    if prompt_own > prompt_rows:
        room = ((0, prompt_own - prompt_rows), (0, 0))
        prompt_query, prompt_output, prompt_output_gradient = (
            jnp.pad(array, room)
            for array in (prompt_query, prompt_output, prompt_output_gradient)
        )
    own_rows = reply_own + prompt_own
    row_width = 2 * GROUP_WIDTH + HEAD_WIDTH

    rows = call(
        prepare_rows,
        "prepare_rows",
        LARGE_MIB,
        (
            place,
            token,
            prompt_query,
            prompt_output,
            prompt_output_gradient,
            reply_query[0],
            reply_output[0],
            reply_output_gradient[0],
        ),
        [shape(LOCAL_HEADS, own_rows, row_width)] + [shape(own_rows, row_width)] * LOCAL_HEADS,
        spec=HBM,
        scratch_shapes=[
            pltpu.VMEM((KEY_VALUE_HEADS, rows, GROUP_WIDTH), BF16)
            for rows in [prompt_own] * 3 + [reply_own] * 3
        ]
        + [pltpu.SemaphoreType.DMA((KEY_VALUE_HEADS * 6,))],
        cost_estimate=pl.CostEstimate(
            flops=6 * reply_own * reply_own * QUERY_HEADS * HEAD_WIDTH,
            bytes_accessed=20 * reply_own * QUERY_HEADS * HEAD_WIDTH,
            transcendentals=0,
        ),
    )

    blocks0, rows, mine1 = lax.optimization_barrier((blocks0, rows, mine1))
    if relayed:
        blocks0[3, 0] = move(blocks0[1, 0], 2)
        blocks0[3, 1] = move(blocks0[2, 1], 1)
    chip1 = jnp.stack([mine1, blocks0[0, 1][1]])
    blocks1 = [chip1] + [move(chip1, away) for away in range(1, chips)]

    blocks = (chips * chip_prompt + RESP_DEV * chips * positions) // block
    slots = (chips * chip_prompt + chips * positions) // block
    all_rows = max(GROUP * positions, -(-GROUP * CORES * prompt_own // 128) * 128)
    sizes = (chips, reply_own, prompt_own, prompt_rows, prompt_keys)
    score_count = GROUP * (positions * RESP_DEV * slots * block)

    cut_rows = prompt_keys // groups
    rows_theirs, *rows_mine = rows
    rows_theirs = swap(rows_theirs)

    def run_attend(local, key_blocks):
        joint_keys = local == 1
        sums = [shape(CORES, *key_shape)] * chips
        if joint_keys:
            sums = [shape(CORES, n, 2 * HEAD_WIDTH) for n in [reply_own] * chips + [prompt_keys] * chips]
        query_mine, query_theirs, *sums = call(
            functools.partial(attend, sizes, joint_keys),
            "attend",
            VMEM_MIB,
            (
                place,
                reply_len,
                reply_slot,
                rows_mine[local],
                rows_theirs,
                *key_blocks,
            ),
            [shape(own_rows, GROUP_WIDTH)] * CORES + sums,
            scalars=3,
            scratch_shapes=[
                pltpu.VMEM((blocks * block, 2 * HEAD_WIDTH), BF16),
                pltpu.VMEM((blocks, HEAD_WIDTH, block), BF16),
                pltpu.VMEM((blocks * block, 2 * HEAD_WIDTH), F32),
                pltpu.VMEM((all_rows, HEAD_WIDTH), BF16),
                pltpu.VMEM((all_rows, HEAD_WIDTH), BF16),
                pltpu.VMEM((HEAD_WIDTH, all_rows), BF16),
                pltpu.VMEM((HEAD_WIDTH, all_rows), BF16),
                pltpu.VMEM((CORES, 8, own_rows), F32),
                pltpu.VMEM((8, all_rows), F32),
                pltpu.VMEM((slots, block, all_rows), F32),
                pltpu.VMEM((slots, block // PART, 8, all_rows), F32),
                pltpu.VMEM((8, all_rows), F32),
                pltpu.VMEM((8, all_rows), F32),
                pltpu.VMEM((HEAD_WIDTH, all_rows), F32),
            ]
            + [pltpu.VMEM((block, all_rows), BF16)] * 4,
            cost_estimate=pl.CostEstimate(
                flops=score_count * 10 * HEAD_WIDTH,
                bytes_accessed=8 * 1024 * 1024,
                transcendentals=2 * score_count,
            ),
        )
        return query_mine, query_theirs, sums

    query_mine0, query_theirs0, sums0 = run_attend(
        0, [blocks0[away, other] for away in range(chips) for other in range(CORES)]
    )
    arrived0 = [sums0[0]] + [move(sums0[away], away) for away in range(1, chips)]
    query_theirs0 = swap(query_theirs0)
    query_mine1, query_theirs1, sums1 = run_attend(1, blocks1)
    arrived0, query_theirs0, query_theirs1, sums1 = lax.optimization_barrier(
        (arrived0, query_theirs0, query_theirs1, sums1)
    )
    prompt1 = [sums1[chips]] + [move(sums1[chips + away], away) for away in range(1, chips)]
    arrived1 = [sums1[0], move(sums1[1], 1)]
    key_width = KEY_VALUE_HEADS * HEAD_WIDTH
    query_width = QUERY_HEADS * HEAD_WIDTH
    query_theirs1 = swap(query_theirs1)
    prompt1, query_theirs1, sums1[2:chips] = lax.optimization_barrier(
        (prompt1, query_theirs1, sums1[2:chips])
    )
    arrived1 += [move(sums1[away], away) for away in range(2, chips)]
    reply0, theirs0, *cuts = call(
        functools.partial(collect_first, chips),
        "collect_first",
        SMALL_MIB,
        (place, *arrived0, *prompt1),
        [shape(reply_own, 2 * HEAD_WIDTH, dtype=F32), shape(reply_own, 2 * HEAD_WIDTH)]
        + [shape(KEY_VALUE_HEADS, cut_rows, 2 * HEAD_WIDTH)] * groups,
        scratch_shapes=[pltpu.VMEM((KEY_VALUE_HEADS, prompt_keys, 2 * HEAD_WIDTH), F32)],
    )
    slices = [cuts[0]] + [
        lax.ppermute(cuts[shift], "rsp", [(g, (g + shift) % groups) for g in range(groups)])
        for shift in range(1, groups)
    ]
    prompt_dq, reply_dq = call(
        finish_queries,
        "finish_queries",
        SMALL_MIB,
        (place, query_mine0, query_theirs0, query_mine1, query_theirs1),
        [shape(prompt_own, query_width), shape(reply_own, query_width)],
        cost_estimate=pl.CostEstimate(
            flops=2 * reply_own * reply_own * query_width,
            bytes_accessed=8 * reply_own * query_width,
            transcendentals=0,
        ),
    )
    slices, prompt_dq, reply_dq = lax.optimization_barrier((slices, prompt_dq, reply_dq))
    reply1, prompts, theirs = call(
        functools.partial(collect_second, chips),
        "collect_second",
        SMALL_MIB,
        (*arrived1, *slices, theirs0),
        [
            shape(reply_own, 2 * HEAD_WIDTH, dtype=F32),
            shape(LOCAL_HEADS, cut_rows, 2 * HEAD_WIDTH, dtype=F32),
            shape(2 * reply_own + 2 * max(cut_rows, 16), 2 * HEAD_WIDTH),
        ],
        scalars=0,
    )
    prompt_dk, prompt_dv, reply_dk, reply_dv = call(
        finish_keys,
        "finish_keys",
        SMALL_MIB,
        (place, reply0, reply1, prompts, swap(theirs)),
        [shape(cut_rows, key_width)] * 2 + [shape(reply_own, key_width)] * 2,
    )
    return (
        prompt_dq[:prompt_rows],
        prompt_dk,
        prompt_dv,
        reply_dq[None],
        reply_dk[None],
        reply_dv[None],
    )


def solution(mesh):
    return jax.shard_map(
        on_device,
        mesh=mesh,
        in_specs=(
            P(("pre", "rsp"), None),
            P("pre", None),
            P("pre", None),
            P(("pre", "rsp"), None),
            P(("pre", "rsp"), None),
            P("rsp", "pre", None),
            P("rsp", "pre", None),
            P("rsp", "pre", None),
            P("rsp", "pre", None),
            P("rsp", "pre", None),
            P(),
            P(),
        ),
        out_specs=(
            P(("pre", "rsp"), None),
            P(("pre", "rsp"), None),
            P(("pre", "rsp"), None),
            P("rsp", "pre", None),
            P("rsp", "pre", None),
            P("rsp", "pre", None),
        ),
        check_vma=False,
    )
```

profile of v0, /device:TPU:0, one launch (start us, length us, event | category | flops | bytes accessed | tf_op | source)
XLA Modules:
  0.0 107.2 jit_solution(2829895932534809651)
XLA Ops:
  0.6 2.4 %prepare_keys.1 = (bf16[384,256]{1,0:T(8,128)(2,1)}, bf16[384,256]{1,0:T(8,128)(2,1)}, bf16[384,256]{1,0:T(8,128)(2,1)}, bf16[2,384,256]{2,1,0:T(8,128)(2,1)}, f32[8,128]{1,0:T(8,128)}) custom-call(bf16[128,512]{1,0:T(8,128)(2,1)} %pk.1, bf16[128,512]{1,0:T(8,128)(2,1)} %pv.1, bf16[256,512]{1,0:T(8,128)(2,1)} %bitcast.15, bf16[256,512]{1,0:T(8,128)(2,1)} %bitcast.16), custom_call_target="tpu_custom_call" | custom-call | tf_op jit(solution)/shard_map/prepare_keys/pallas_call | solution.py:553
  3.6 2.6 %collective-permute-start.1 = (bf16[384,256]{1,0:T(8,128)(2,1)}, bf16[384,256]{1,0:T(8,128)(2,1)S(1)}, u32[]{:S(2)}, u32[]{:S(2)}) collective-permute-start(bf16[384,256]{1,0:T(8,128)(2,1)} %get-tuple-element.92.refs_2_), channel_id=1, source_target_pairs={{0,8},{4,12},{8,0},{12,4},{16,24},{20,28},{24,16},{28,20},{1,9},{5... | collective-permute-start | bytes 589832 | tf_op jit(solution)/shard_map/ppermute | solution.py:547
  6.2 1.5 %collective-permute-start.3 = (bf16[384,256]{1,0:T(8,128)(2,1)}, bf16[384,256]{1,0:T(8,128)(2,1)S(1)}, u32[]{:S(2)}, u32[]{:S(2)}) collective-permute-start(bf16[384,256]{1,0:T(8,128)(2,1)} %get-tuple-element.92.refs_2_), channel_id=1, source_target_pairs={{0,16},{4,20},{8,24},{12,28},{16,0},{20,4},{24,8},{28,12},{1,17},{... | collective-permute-start | bytes 589832 | tf_op jit(solution)/shard_map/ppermute | solution.py:547
  8.0 0.7 pad_add_fusion.place
  8.7 6.5 %prepare_rows.1 = (bf16[2,288,1408]{2,1,0:T(8,128)(2,1)}, bf16[288,1408]{1,0:T(8,128)(2,1)}, bf16[288,1408]{1,0:T(8,128)(2,1)}) custom-call(s32[3]{0:T(128)} %pad_add_fusion.place, f32[8,128]{1,0:T(8,128)} %get-tuple-element.85.token, bf16[32,2560]{1,0:T(8,128)(2,1)} %pq.1, bf16[32,2560]{1,0:T(8,128)(2,1)} %po.1, bf16[32,2560]{1,0:T(8,128)(2,1)} %pg.1, ...), custom_call_target="tpu_custom_call" | custom-call | flops 1006632960 | bytes 13107200 | tf_op jit(solution)/shard_map/prepare_rows/pallas_call | solution.py:553
  15.2 0.6 collective-permute-done.2.refs_5_
  15.8 1.0 collective-permute-done.4.refs_7_
  16.8 0.6 collective-permute-start.5
  17.4 1.5 %collective-permute-start.6 = (bf16[384,256]{1,0:T(8,128)(2,1)S(1)}, bf16[384,256]{1,0:T(8,128)(2,1)S(1)}, u32[]{:S(2)}, u32[]{:S(2)}) collective-permute-start(bf16[384,256]{1,0:T(8,128)(2,1)S(1)} %collective-permute-done.1.refs_4_), channel_id=1, source_target_pairs={{0,16},{4,20},{8,24},{12,28},{16,0},{20,4},{24,8},{28,12},{1,17},{... | collective-permute-start | bytes 589832 | tf_op jit(solution)/shard_map/ppermute | solution.py:547
  18.9 0.5 collective-permute-start.7
  19.5 1.6 %collective-permute-start.12 = (bf16[2,384,256]{2,1,0:T(8,128)(2,1)S(1)}, bf16[2,384,256]{2,1,0:T(8,128)(2,1)S(1)}, u32[]{:S(2)}, u32[]{:S(2)}) collective-permute-start(bf16[2,384,256]{2,1,0:T(8,128)(2,1)S(1)} %pad_maximum_fusion.refs_2_), channel_id=1, source_target_pairs={{0,8},{4,12},{8,0},{12,4},{16,24},{20,28},{24,16},{28,20},{1,9},{5... | collective-permute-start | bytes 1179656 | tf_op jit(solution)/shard_map/ppermute | solution.py:547
  21.6 3.6 %collective-permute-done.6.refs_8_ = bf16[384,256]{1,0:T(8,128)(2,1)S(1)} collective-permute-done((bf16[384,256]{1,0:T(8,128)(2,1)S(1)}, bf16[384,256]{1,0:T(8,128)(2,1)S(1)}, u32[]{:S(2)}, u32[]{:S(2)}) %collective-permute-start.6) | collective-permute-done | bytes 196640 | tf_op jit(solution)/shard_map/ppermute | solution.py:547
  25.2 1.5 %collective-permute-start.14 = (bf16[2,384,256]{2,1,0:T(8,128)(2,1)S(1)}, bf16[2,384,256]{2,1,0:T(8,128)(2,1)S(1)}, u32[]{:S(2)}, u32[]{:S(2)}) collective-permute-start(bf16[2,384,256]{2,1,0:T(8,128)(2,1)S(1)} %pad_maximum_fusion.refs_2_), channel_id=1, source_target_pairs={{0,24},{4,28},{8,16},{12,20},{16,8},{20,12},{24,0},{28,4},{1,25},{... | collective-permute-start | bytes 1179656 | tf_op jit(solution)/shard_map/ppermute | solution.py:547
  26.8 1.1 %copy-done.2 = bf16[288,1408]{1,0:T(8,128)(2,1)S(1)} copy-done((bf16[288,1408]{1,0:T(8,128)(2,1)S(1)}, bf16[288,1408]{1,0:T(8,128)(2,1)}, u32[]{:S(2)}) %copy-start.2) | copy-done | bytes 811032
  27.9 16.9 %attend.2 = (bf16[288,640]{1,0:T(8,128)(2,1)S(1)}, bf16[288,640]{1,0:T(8,128)(2,1)S(1)}, bf16[2,384,256]{2,1,0:T(8,128)(2,1)S(1)}, bf16[2,384,256]{2,1,0:T(8,128...) custom-call(s32[3]{0:T(128)S(1)} %copy-done, s32[8]{0:T(128)S(1)} %copy-done.4, ...), custom_call_target="tpu_custom_call" | custom-call | flops 6710886400 | bytes 8388608 | tf_op jit(solution)/shard_map/attend/pallas_call | solution.py:553
  44.8 3.5 %collective-permute-start.8 = (bf16[2,384,256]{2,1,0:T(8,128)(2,1)S(1)}, bf16[2,384,256]{2,1,0:T(8,128)(2,1)S(1)}, u32[]{:S(2)}, u32[]{:S(2)}) collective-permute-start(bf16[2,384,256]{2,1,0:T(8,128)(2,1)S(1)} %get-tuple-element.99), channel_id=1, source_target_pairs={{0,8},{4,12},{8,0},{12,4},{16,24},{20,28},{24,16},{28,20},{1,9},{5... | collective-permute-start | bytes 1179656 | tf_op jit(solution)/shard_map/ppermute | solution.py:547
  48.3 5.8 %collective-permute-start.9 = (bf16[2,384,256]{2,1,0:T(8,128)(2,1)S(1)}, bf16[2,384,256]{2,1,0:T(8,128)(2,1)S(1)}, u32[]{:S(2)}, u32[]{:S(2)}) collective-permute-start(bf16[2,384,256]{2,1,0:T(8,128)(2,1)S(1)} %get-tuple-element.100), channel_id=1, source_target_pairs={{0,16},{4,20},{8,24},{12,28},{16,0},{20,4},{24,8},{28,12},{1,17},{... | collective-permute-start | bytes 1179656 | tf_op jit(solution)/shard_map/ppermute | solution.py:547
  54.2 16.8 %attend.3 = (bf16[288,640]{1,0:T(8,128)(2,1)S(1)}, bf16[288,640]{1,0:T(8,128)(2,1)S(1)}, bf16[2,256,256]{2,1,0:T(8,128)(2,1)S(1)}, bf16[2,256,256]{2,1,0:T(8,128...) custom-call(s32[3]{0:T(128)S(1)} %copy-done, ...), custom_call_target="tpu_custom_call" | custom-call | flops 6710886400 | bytes 8388608 | tf_op jit(solution)/shard_map/attend/pallas_call | solution.py:553
  71.0 0.5 collective-permute-start.18
  71.6 3.4 %collective-permute-start.15 = (bf16[2,128,256]{2,1,0:T(8,128)(2,1)S(1)}, bf16[2,128,256]{2,1,0:T(8,128)(2,1)S(1)}, u32[]{:S(2)}, u32[]{:S(2)}) collective-permute-start(bf16[2,128,256]{2,1,0:T(8,128)(2,1)S(1)} %get-tuple-element.119), channel_id=1, source_target_pairs={{0,8},{4,12},{8,0},{12,4},{16,24},{20,28},{24,16},{28,20},{1,9},{5... | collective-permute-start | bytes 393224 | tf_op jit(solution)/shard_map/ppermute | solution.py:547
  74.9 7.3 %collective-permute-start.16 = (bf16[2,128,256]{2,1,0:T(8,128)(2,1)S(1)}, bf16[2,128,256]{2,1,0:T(8,128)(2,1)S(1)}, u32[]{:S(2)}, u32[]{:S(2)}) collective-permute-start(bf16[2,128,256]{2,1,0:T(8,128)(2,1)S(1)} %get-tuple-element.120), channel_id=1, source_target_pairs={{0,16},{4,20},{8,24},{12,28},{16,0},{20,4},{24,8},{28,12},{1,17},{... | collective-permute-start | bytes 393224 | tf_op jit(solution)/shard_map/ppermute | solution.py:547
  82.2 1.5 %collective-permute-start.22 = (bf16[2,256,256]{2,1,0:T(8,128)(2,1)S(1)}, bf16[2,256,256]{2,1,0:T(8,128)(2,1)S(1)}, u32[]{:S(2)}, u32[]{:S(2)}) collective-permute-start(bf16[2,256,256]{2,1,0:T(8,128)(2,1)S(1)} %get-tuple-element.142), channel_id=1, source_target_pairs={{0,8},{4,12},{8,0},{12,4},{16,24},{20,28},{24,16},{28,20},{1,9},{5... | collective-permute-start | bytes 786440 | tf_op jit(solution)/shard_map/ppermute | solution.py:547
  83.7 4.1 %collective-permute-done.16.refs_6_ = bf16[2,128,256]{2,1,0:T(8,128)(2,1)S(1)} collective-permute-done((bf16[2,128,256]{2,1,0:T(8,128)(2,1)S(1)}, bf16[2,128,256]{2,1,0:T(8,128)(2,1)S(1)}, u32[]{:S(2)}, u32[]{:S(2)}) %collective-permute-start.16) | collective-permute-done | bytes 131104 | tf_op jit(solution)/shard_map/ppermute | solution.py:547
  87.8 1.8 %collective-permute-done.17.refs_7_ = bf16[2,128,256]{2,1,0:T(8,128)(2,1)S(1)} collective-permute-done((bf16[2,128,256]{2,1,0:T(8,128)(2,1)S(1)}, bf16[2,128,256]{2,1,0:T(8,128)(2,1)S(1)}, u32[]{:S(2)}, u32[]{:S(2)}) %collective-permute-start.17) | collective-permute-done | bytes 131104 | tf_op jit(solution)/shard_map/ppermute | solution.py:547
  89.6 0.7 collective-permute-start.23
  90.2 2.0 %collective-permute-start.24 = (bf16[2,256,256]{2,1,0:T(8,128)(2,1)S(1)}, bf16[2,256,256]{2,1,0:T(8,128)(2,1)S(1)}, u32[]{:S(2)}, u32[]{:S(2)}) collective-permute-start(bf16[2,256,256]{2,1,0:T(8,128)(2,1)S(1)} %get-tuple-element.144), channel_id=1, source_target_pairs={{0,24},{4,28},{8,16},{12,20},{16,8},{20,12},{24,0},{28,4},{1,25},{... | collective-permute-start | bytes 786440 | tf_op jit(solution)/shard_map/ppermute | solution.py:547
  92.3 0.9 collect_first.1
  93.3 6.1 %collective-permute-done.19.refs_5_ = bf16[4,32,256]{2,1,0:T(8,128)(2,1)S(1)} collective-permute-done((bf16[4,32,256]{2,1,0:T(8,128)(2,1)S(1)}, bf16[4,32,256]{2,1,0:T(8,128)(2,1)S(1)}, u32[]{:S(2)}, u32[]{:S(2)}) %collective-permute-start.19) | collective-permute-done | bytes 65568 | tf_op jit(solution)/shard_map/ppermute | solution.py:709
  99.4 2.2 %finish_queries.1 = (bf16[32,2560]{1,0:T(8,128)(2,1)}, bf16[256,2560]{1,0:T(8,128)(2,1)}) custom-call(s32[3]{0:T(128)S(1)} %copy-done, bf16[288,640]{1,0:T(8,128)(2,1)S(1)} %get-tuple-element.133.refs_0_, bf16[288,640]{1,0:T(8,128)(2,1)S(1)} %collective-permute-done.11.refs_1_, bf16[288,640]{1,0:T(8,128)(2,1)S(1)} %get-tuple-element.135.refs_2_, ...), custom_call_target="tpu_custom_call" | custom-call | flops 335544320 | bytes 5242880 | tf_op jit(solution)/shard_map/finish_queries/pallas_call | solution.py:553
  101.6 2.1 %collective-permute-done.21.refs_7_ = bf16[4,32,256]{2,1,0:T(8,128)(2,1)S(1)} collective-permute-done((bf16[4,32,256]{2,1,0:T(8,128)(2,1)S(1)}, bf16[4,32,256]{2,1,0:T(8,128)(2,1)S(1)}, u32[]{:S(2)}, u32[]{:S(2)}) %collective-permute-start.21) | collective-permute-done | bytes 65568 | tf_op jit(solution)/shard_map/ppermute | solution.py:709
  103.9 1.6 %collective-permute-done.25.theirs = bf16[576,256]{1,0:T(8,128)(2,1)S(1)} collective-permute-done((bf16[576,256]{1,0:T(8,128)(2,1)S(1)}, bf16[576,256]{1,0:T(8,128)(2,1)S(1)}, u32[]{:S(2)}, u32[]{:S(2)}) %collective-permute-start.25) | collective-permute-done | bytes 294944 | tf_op jit(solution)/shard_map/ppermute | solution.py:547
  105.5 1.7 %finish_keys.1 = (bf16[32,512]{1,0:T(8,128)(2,1)}, bf16[32,512]{1,0:T(8,128)(2,1)}, bf16[256,512]{1,0:T(8,128)(2,1)}, bf16[256,512]{1,0:T(8,128)(2,1)}) custom-call(s32[3]{0:T(128)S(1)} %copy-done, f32[256,256]{1,0:T(8,128)S(1)} %get-tuple-element.140.reply0, f32[256,256]{1,0:T(8,128)S(1)} %get-tuple-element.150.reply1, ...), custom_call_target="tpu_custom_call" | custom-call | tf_op jit(solution)/shard_map/finish_keys/pallas_call | solution.py:553
  (45 shorter events, 2.0 us)
Async XLA Ops:
  3.1 13.7 %collective-permute-start = (bf16[2,384,256]{2,1,0:T(8,128)(2,1)}, bf16[2,384,256]{2,1,0:T(8,128)(2,1)S(1)}, u32[]{:S(2)}, u32[]{:S(2)}) collective-permute-start(bf16[2,384,256]{2,1,0:T(8,128)(2,1)} %get-tuple-element.83), channel_id=1, source_target_pairs={{0,4},{4,0},{8,12},{12,8},{16,20},{20,16},{24,28},{28,24},{1,5},{5... | collective-permute-start | bytes 1179656 | tf_op jit(solution)/shard_map/ppermute | solution.py:547
  3.6 11.6 %collective-permute-start.1 = (bf16[384,256]{1,0:T(8,128)(2,1)}, bf16[384,256]{1,0:T(8,128)(2,1)S(1)}, u32[]{:S(2)}, u32[]{:S(2)}) collective-permute-start(bf16[384,256]{1,0:T(8,128)(2,1)} %get-tuple-element.92.refs_2_), channel_id=1, source_target_pairs={{0,8},{4,12},{8,0},{12,4},{16,24},{20,28},{24,16},{28,20},{1,9},{5... | collective-permute-start | bytes 589832 | tf_op jit(solution)/shard_map/ppermute | solution.py:547
  6.2 9.7 %collective-permute-start.3 = (bf16[384,256]{1,0:T(8,128)(2,1)}, bf16[384,256]{1,0:T(8,128)(2,1)S(1)}, u32[]{:S(2)}, u32[]{:S(2)}) collective-permute-start(bf16[384,256]{1,0:T(8,128)(2,1)} %get-tuple-element.92.refs_2_), channel_id=1, source_target_pairs={{0,16},{4,20},{8,24},{12,28},{16,0},{20,4},{24,8},{28,12},{1,17},{... | collective-permute-start | bytes 589832 | tf_op jit(solution)/shard_map/ppermute | solution.py:547
  7.7 8.1 %collective-permute-start.2 = (bf16[384,256]{1,0:T(8,128)(2,1)}, bf16[384,256]{1,0:T(8,128)(2,1)S(1)}, u32[]{:S(2)}, u32[]{:S(2)}) collective-permute-start(bf16[384,256]{1,0:T(8,128)(2,1)} %get-tuple-element.84), channel_id=1, source_target_pairs={{0,12},{4,8},{8,4},{12,0},{16,28},{20,24},{24,20},{28,16},{1,13},{... | collective-permute-start | bytes 589832 | tf_op jit(solution)/shard_map/ppermute | solution.py:547
  7.7 9.1 %collective-permute-start.4 = (bf16[384,256]{1,0:T(8,128)(2,1)}, bf16[384,256]{1,0:T(8,128)(2,1)S(1)}, u32[]{:S(2)}, u32[]{:S(2)}) collective-permute-start(bf16[384,256]{1,0:T(8,128)(2,1)} %get-tuple-element.84), channel_id=1, source_target_pairs={{0,20},{4,16},{8,28},{12,24},{16,4},{20,0},{24,12},{28,8},{1,21},{... | collective-permute-start | bytes 589832 | tf_op jit(solution)/shard_map/ppermute | solution.py:547
  8.7 10.8 %copy-start.6 = (bf16[384,256]{1,0:T(8,128)(2,1)S(1)}, bf16[384,256]{1,0:T(8,128)(2,1)}, u32[]{:S(2)}) copy-start(bf16[384,256]{1,0:T(8,128)(2,1)} %get-tuple-element.104) | copy-start | bytes 589828
  8.7 18.1 %copy-start = (s32[3]{0:T(128)S(1)}, s32[3]{0:T(128)}, u32[]{:S(2)}) copy-start(s32[3]{0:T(128)} %pad_add_fusion.place) | copy-start | bytes 40
  8.7 18.1 %copy-start.3 = (bf16[384,256]{1,0:T(8,128)(2,1)S(1)}, bf16[384,256]{1,0:T(8,128)(2,1)}, u32[]{:S(2)}) copy-start(bf16[384,256]{1,0:T(8,128)(2,1)} %get-tuple-element.92.refs_2_) | copy-start | bytes 589828
  8.7 18.1 %copy-start.4 = (s32[8]{0:T(128)S(1)}, s32[8]{0:T(128)}, u32[]{:S(2)}) copy-start(s32[8]{0:T(128)} %reply_len.3) | copy-start | bytes 100
  8.7 18.1 %copy-start.5 = (s32[8]{0:T(128)S(1)}, s32[8]{0:T(128)}, u32[]{:S(2)}) copy-start(s32[8]{0:T(128)} %reply_slot.3) | copy-start | bytes 100
  16.8 9.9 %collective-permute-start.5 = (bf16[2,288,1408]{2,1,0:T(8,128)(2,1)}, bf16[2,288,1408]{2,1,0:T(8,128)(2,1)S(1)}, u32[]{:S(2)}, u32[]{:S(2)}) collective-permute-start(bf16[2,288,1408]{2,1,0:T(8,128)(2,1)} %get-tuple-element.91), channel_id=1, source_target_pairs={{0,4},{4,0},{8,12},{12,8},{16,20},{20,16},{24,28},{28,24},{1,5},{5... | collective-permute-start | bytes 4866056 | tf_op jit(solution)/shard_map/ppermute | solution.py:547
  17.4 7.8 %collective-permute-start.6 = (bf16[384,256]{1,0:T(8,128)(2,1)S(1)}, bf16[384,256]{1,0:T(8,128)(2,1)S(1)}, u32[]{:S(2)}, u32[]{:S(2)}) collective-permute-start(bf16[384,256]{1,0:T(8,128)(2,1)S(1)} %collective-permute-done.1.refs_4_), channel_id=1, source_target_pairs={{0,16},{4,20},{8,24},{12,28},{16,0},{20,4},{24,8},{28,12},{1,17},{... | collective-permute-start | bytes 589832 | tf_op jit(solution)/shard_map/ppermute | solution.py:547
  18.9 7.8 %collective-permute-start.7 = (bf16[384,256]{1,0:T(8,128)(2,1)S(1)}, bf16[384,256]{1,0:T(8,128)(2,1)S(1)}, u32[]{:S(2)}, u32[]{:S(2)}) collective-permute-start(bf16[384,256]{1,0:T(8,128)(2,1)S(1)} %collective-permute-done.4.refs_7_), channel_id=1, source_target_pairs={{0,8},{4,12},{8,0},{12,4},{16,24},{20,28},{24,16},{28,20},{1,9},{5... | collective-permute-start | bytes 589832 | tf_op jit(solution)/shard_map/ppermute | solution.py:547
  19.5 34.7 %copy-start.1 = (bf16[288,1408]{1,0:T(8,128)(2,1)S(1)}, bf16[288,1408]{1,0:T(8,128)(2,1)}, u32[]{:S(2)}) copy-start(bf16[288,1408]{1,0:T(8,128)(2,1)} %get-tuple-element.103.refs_0_) | copy-start | bytes 2433028
  19.5 34.5 %collective-permute-start.12 = (bf16[2,384,256]{2,1,0:T(8,128)(2,1)S(1)}, bf16[2,384,256]{2,1,0:T(8,128)(2,1)S(1)}, u32[]{:S(2)}, u32[]{:S(2)}) collective-permute-start(bf16[2,384,256]{2,1,0:T(8,128)(2,1)S(1)} %pad_maximum_fusion.refs_2_), channel_id=1, source_target_pairs={{0,8},{4,12},{8,0},{12,4},{16,24},{20,28},{24,16},{28,20},{1,9},{5... | collective-permute-start | bytes 1179656 | tf_op jit(solution)/shard_map/ppermute | solution.py:547
  21.1 33.0 %collective-permute-start.13 = (bf16[2,384,256]{2,1,0:T(8,128)(2,1)S(1)}, bf16[2,384,256]{2,1,0:T(8,128)(2,1)S(1)}, u32[]{:S(2)}, u32[]{:S(2)}) collective-permute-start(bf16[2,384,256]{2,1,0:T(8,128)(2,1)S(1)} %pad_maximum_fusion.refs_2_), channel_id=1, source_target_pairs={{0,16},{4,20},{8,24},{12,28},{16,0},{20,4},{24,8},{28,12},{1,17},{... | collective-permute-start | bytes 1179656 | tf_op jit(solution)/shard_map/ppermute | solution.py:547
  25.2 29.0 %collective-permute-start.14 = (bf16[2,384,256]{2,1,0:T(8,128)(2,1)S(1)}, bf16[2,384,256]{2,1,0:T(8,128)(2,1)S(1)}, u32[]{:S(2)}, u32[]{:S(2)}) collective-permute-start(bf16[2,384,256]{2,1,0:T(8,128)(2,1)S(1)} %pad_maximum_fusion.refs_2_), channel_id=1, source_target_pairs={{0,24},{4,28},{8,16},{12,20},{16,8},{20,12},{24,0},{28,4},{1,25},{... | collective-permute-start | bytes 1179656 | tf_op jit(solution)/shard_map/ppermute | solution.py:547
  44.8 26.2 %collective-permute-start.8 = (bf16[2,384,256]{2,1,0:T(8,128)(2,1)S(1)}, bf16[2,384,256]{2,1,0:T(8,128)(2,1)S(1)}, u32[]{:S(2)}, u32[]{:S(2)}) collective-permute-start(bf16[2,384,256]{2,1,0:T(8,128)(2,1)S(1)} %get-tuple-element.99), channel_id=1, source_target_pairs={{0,8},{4,12},{8,0},{12,4},{16,24},{20,28},{24,16},{28,20},{1,9},{5... | collective-permute-start | bytes 1179656 | tf_op jit(solution)/shard_map/ppermute | solution.py:547
  48.3 22.7 %collective-permute-start.9 = (bf16[2,384,256]{2,1,0:T(8,128)(2,1)S(1)}, bf16[2,384,256]{2,1,0:T(8,128)(2,1)S(1)}, u32[]{:S(2)}, u32[]{:S(2)}) collective-permute-start(bf16[2,384,256]{2,1,0:T(8,128)(2,1)S(1)} %get-tuple-element.100), channel_id=1, source_target_pairs={{0,16},{4,20},{8,24},{12,28},{16,0},{20,4},{24,8},{28,12},{1,17},{... | collective-permute-start | bytes 1179656 | tf_op jit(solution)/shard_map/ppermute | solution.py:547
  54.1 16.9 %collective-permute-start.10 = (bf16[2,384,256]{2,1,0:T(8,128)(2,1)S(1)}, bf16[2,384,256]{2,1,0:T(8,128)(2,1)S(1)}, u32[]{:S(2)}, u32[]{:S(2)}) collective-permute-start(bf16[2,384,256]{2,1,0:T(8,128)(2,1)S(1)} %get-tuple-element.101), channel_id=1, source_target_pairs={{0,24},{4,28},{8,16},{12,20},{16,8},{20,12},{24,0},{28,4},{1,25},{... | collective-permute-start | bytes 1179656 | tf_op jit(solution)/shard_map/ppermute | solution.py:547
  54.1 16.9 %collective-permute-start.11 = (bf16[288,640]{1,0:T(8,128)(2,1)S(1)}, bf16[288,640]{1,0:T(8,128)(2,1)S(1)}, u32[]{:S(2)}, u32[]{:S(2)}) collective-permute-start(bf16[288,640]{1,0:T(8,128)(2,1)S(1)} %get-tuple-element.102), channel_id=1, source_target_pairs={{0,4},{4,0},{8,12},{12,8},{16,20},{20,16},{24,28},{28,24},{1,5},{5... | collective-permute-start | bytes 1105928 | tf_op jit(solution)/shard_map/ppermute | solution.py:547
  71.0 18.5 %collective-permute-start.18 = (bf16[288,640]{1,0:T(8,128)(2,1)S(1)}, bf16[288,640]{1,0:T(8,128)(2,1)S(1)}, u32[]{:S(2)}, u32[]{:S(2)}) collective-permute-start(bf16[288,640]{1,0:T(8,128)(2,1)S(1)} %get-tuple-element.122), channel_id=1, source_target_pairs={{0,4},{4,0},{8,12},{12,8},{16,20},{20,16},{24,28},{28,24},{1,5},{5... | collective-permute-start | bytes 1105928 | tf_op jit(solution)/shard_map/ppermute | solution.py:547
  71.6 12.1 %collective-permute-start.15 = (bf16[2,128,256]{2,1,0:T(8,128)(2,1)S(1)}, bf16[2,128,256]{2,1,0:T(8,128)(2,1)S(1)}, u32[]{:S(2)}, u32[]{:S(2)}) collective-permute-start(bf16[2,128,256]{2,1,0:T(8,128)(2,1)S(1)} %get-tuple-element.119), channel_id=1, source_target_pairs={{0,8},{4,12},{8,0},{12,4},{16,24},{20,28},{24,16},{28,20},{1,9},{5... | collective-permute-start | bytes 393224 | tf_op jit(solution)/shard_map/ppermute | solution.py:547
  74.9 12.8 %collective-permute-start.16 = (bf16[2,128,256]{2,1,0:T(8,128)(2,1)S(1)}, bf16[2,128,256]{2,1,0:T(8,128)(2,1)S(1)}, u32[]{:S(2)}, u32[]{:S(2)}) collective-permute-start(bf16[2,128,256]{2,1,0:T(8,128)(2,1)S(1)} %get-tuple-element.120), channel_id=1, source_target_pairs={{0,16},{4,20},{8,24},{12,28},{16,0},{20,4},{24,8},{28,12},{1,17},{... | collective-permute-start | bytes 393224 | tf_op jit(solution)/shard_map/ppermute | solution.py:547
  82.2 7.3 %collective-permute-start.17 = (bf16[2,128,256]{2,1,0:T(8,128)(2,1)S(1)}, bf16[2,128,256]{2,1,0:T(8,128)(2,1)S(1)}, u32[]{:S(2)}, u32[]{:S(2)}) collective-permute-start(bf16[2,128,256]{2,1,0:T(8,128)(2,1)S(1)} %get-tuple-element.121), channel_id=1, source_target_pairs={{0,24},{4,28},{8,16},{12,20},{16,8},{20,12},{24,0},{28,4},{1,25},{... | collective-permute-start | bytes 393224 | tf_op jit(solution)/shard_map/ppermute | solution.py:547
  82.2 21.4 %collective-permute-start.22 = (bf16[2,256,256]{2,1,0:T(8,128)(2,1)S(1)}, bf16[2,256,256]{2,1,0:T(8,128)(2,1)S(1)}, u32[]{:S(2)}, u32[]{:S(2)}) collective-permute-start(bf16[2,256,256]{2,1,0:T(8,128)(2,1)S(1)} %get-tuple-element.142), channel_id=1, source_target_pairs={{0,8},{4,12},{8,0},{12,4},{16,24},{20,28},{24,16},{28,20},{1,9},{5... | collective-permute-start | bytes 786440 | tf_op jit(solution)/shard_map/ppermute | solution.py:547
  89.6 14.1 %collective-permute-start.23 = (bf16[2,256,256]{2,1,0:T(8,128)(2,1)S(1)}, bf16[2,256,256]{2,1,0:T(8,128)(2,1)S(1)}, u32[]{:S(2)}, u32[]{:S(2)}) collective-permute-start(bf16[2,256,256]{2,1,0:T(8,128)(2,1)S(1)} %get-tuple-element.143), channel_id=1, source_target_pairs={{0,16},{4,20},{8,24},{12,28},{16,0},{20,4},{24,8},{28,12},{1,17},{... | collective-permute-start | bytes 786440 | tf_op jit(solution)/shard_map/ppermute | solution.py:547
  90.2 13.4 %collective-permute-start.24 = (bf16[2,256,256]{2,1,0:T(8,128)(2,1)S(1)}, bf16[2,256,256]{2,1,0:T(8,128)(2,1)S(1)}, u32[]{:S(2)}, u32[]{:S(2)}) collective-permute-start(bf16[2,256,256]{2,1,0:T(8,128)(2,1)S(1)} %get-tuple-element.144), channel_id=1, source_target_pairs={{0,24},{4,28},{8,16},{12,20},{16,8},{20,12},{24,0},{28,4},{1,25},{... | collective-permute-start | bytes 786440 | tf_op jit(solution)/shard_map/ppermute | solution.py:547
  93.2 6.2 %collective-permute-start.19 = (bf16[4,32,256]{2,1,0:T(8,128)(2,1)S(1)}, bf16[4,32,256]{2,1,0:T(8,128)(2,1)S(1)}, u32[]{:S(2)}, u32[]{:S(2)}) collective-permute-start(bf16[4,32,256]{2,1,0:T(8,128)(2,1)S(1)} %get-tuple-element.130), channel_id=1, source_target_pairs={{0,1},{1,2},{2,3},{3,0},{4,5},{5,6},{6,7},{7,4},{8,9},{9,10},{10,1... | collective-permute-start | bytes 196616 | tf_op jit(solution)/shard_map/ppermute | solution.py:709
  93.3 8.3 %collective-permute-start.20 = (bf16[4,32,256]{2,1,0:T(8,128)(2,1)S(1)}, bf16[4,32,256]{2,1,0:T(8,128)(2,1)S(1)}, u32[]{:S(2)}, u32[]{:S(2)}) collective-permute-start(bf16[4,32,256]{2,1,0:T(8,128)(2,1)S(1)} %get-tuple-element.131), channel_id=1, source_target_pairs={{0,2},{1,3},{2,0},{3,1},{4,6},{5,7},{6,4},{7,5},{8,10},{9,11},{10,... | collective-permute-start | bytes 196616 | tf_op jit(solution)/shard_map/ppermute | solution.py:709
  99.4 4.3 %collective-permute-start.21 = (bf16[4,32,256]{2,1,0:T(8,128)(2,1)S(1)}, bf16[4,32,256]{2,1,0:T(8,128)(2,1)S(1)}, u32[]{:S(2)}, u32[]{:S(2)}) collective-permute-start(bf16[4,32,256]{2,1,0:T(8,128)(2,1)S(1)} %get-tuple-element.132), channel_id=1, source_target_pairs={{0,3},{1,0},{2,1},{3,2},{4,7},{5,4},{6,5},{7,6},{8,11},{9,8},{10,9... | collective-permute-start | bytes 196616 | tf_op jit(solution)/shard_map/ppermute | solution.py:709
  103.9 1.6 %collective-permute-start.25 = (bf16[576,256]{1,0:T(8,128)(2,1)S(1)}, bf16[576,256]{1,0:T(8,128)(2,1)S(1)}, u32[]{:S(2)}, u32[]{:S(2)}) collective-permute-start(bf16[576,256]{1,0:T(8,128)(2,1)S(1)} %get-tuple-element.152), channel_id=1, source_target_pairs={{0,4},{4,0},{8,12},{12,8},{16,20},{20,16},{24,28},{28,24},{1,5},{5... | collective-permute-start | bytes 884744 | tf_op jit(solution)/shard_map/ppermute | solution.py:547
  (1 other events, 1.1 us)
where the time goes:
time: 107 us
  Pallas kernels  47.5 us (44%)
  starting transfers between devices  36 us (34%)
  waiting for transfers between devices  20.9 us (20%)
  local copies, waits for them, and re-layouts  1.18 us (1%)
    pallas_call x8, Pallas kernels, call(): pl.pallas_call(kernel, out_shape=outs, in_specs=[SMEM] * scalars + [spec]...  47.5 us
    ppermute x23, starting transfers between devices, move(): return lax.ppermute(array, 'pre', pairs)  35.9 us
    ppermute x23, waiting for transfers between devices, move(): return lax.ppermute(array, 'pre', pairs)  12.7 us
    ppermute x3, waiting for transfers between devices, on_device(): lax.ppermute(cuts[shift], 'rsp', [(g, (g + shift) % groups) for g in rang...  8.16 us
  transfers between devices with their start and end apart: 26, of which 9 were waited for; matrix products, arithmetic and copies ran while one was open for 1% of the time, Pallas kernels for 40%

commit v1 on v0

--- a/solution.py
+++ b/solution.py
@@ -621,6 +621,8 @@
     if relayed:
         blocks0[3, 0] = move(blocks0[1, 0], 2)
         blocks0[3, 1] = move(blocks0[2, 1], 1)
+    rows_theirs, *rows_mine = rows
+    rows_theirs, mine1 = lax.optimization_barrier((swap(rows_theirs), mine1))
     chip1 = jnp.stack([mine1, blocks0[0, 1][1]])
     blocks1 = [chip1] + [move(chip1, away) for away in range(1, chips)]
 
@@ -631,9 +633,6 @@
     score_count = GROUP * (positions * RESP_DEV * slots * block)
 
     cut_rows = prompt_keys // groups
-    rows_theirs, *rows_mine = rows
-    rows_theirs = swap(rows_theirs)
-
     def run_attend(local, key_blocks):
         joint_keys = local == 1
         sums = [shape(CORES, *key_shape)] * chips
@@ -688,14 +687,11 @@
         (arrived0, query_theirs0, query_theirs1, sums1)
     )
     prompt1 = [sums1[chips]] + [move(sums1[chips + away], away) for away in range(1, chips)]
-    arrived1 = [sums1[0], move(sums1[1], 1)]
     key_width = KEY_VALUE_HEADS * HEAD_WIDTH
     query_width = QUERY_HEADS * HEAD_WIDTH
     query_theirs1 = swap(query_theirs1)
-    prompt1, query_theirs1, sums1[2:chips] = lax.optimization_barrier(
-        (prompt1, query_theirs1, sums1[2:chips])
-    )
-    arrived1 += [move(sums1[away], away) for away in range(2, chips)]
+    prompt1, query_theirs1, sums1 = lax.optimization_barrier((prompt1, query_theirs1, sums1[:chips]))
+    arrived1 = [sums1[0]] + [move(sums1[away], away) for away in range(1, chips)]
     reply0, theirs0, *cuts = call(
         functools.partial(collect_first, chips),
         "collect_first",

time: 107 us -> 105 us (0.981); the launches traced: 107 us -> 103 us
  starting transfers between devices: 36 us -> 31.2 us
    ppermute x23, starting transfers between devices: 35.9 us -> 31.1 us  [move(): return lax.ppermute(array, 'pre', pairs)]
  transfers between devices with their start and end apart: 26 -> 26, of which waited for: 9 -> 10; matrix products, arithmetic and copies ran while one was open for 1% -> 1% of each run, Pallas kernels for 40% -> 42%
where the time goes in v1:
time: 105 us; the launch traced here: 103 us
  Pallas kernels  47.5 us (45%)
  starting transfers between devices  31.2 us (30%)
  waiting for transfers between devices  21.9 us (21%)
  local copies, waits for them, and re-layouts  1.18 us (1%)
    pallas_call x8, Pallas kernels, call(): pl.pallas_call(kernel, out_shape=outs, in_specs=[SMEM] * scalars + [spec]...  47.5 us
    ppermute x23, starting transfers between devices, move(): return lax.ppermute(array, 'pre', pairs)  31.1 us
    ppermute x23, waiting for transfers between devices, move(): return lax.ppermute(array, 'pre', pairs)  13.8 us
    ppermute x3, waiting for transfers between devices, on_device(): lax.ppermute(cuts[shift], 'rsp', [(g, (g + shift) % groups) for g in rang...  8.15 us
  transfers between devices with their start and end apart: 26, of which 10 were waited for; matrix products, arithmetic and copies ran while one was open for 1% of the time, Pallas kernels for 42%

profile of v1, /device:TPU:0, one launch (start us, length us, event | category | flops | bytes accessed | tf_op | source)
XLA Modules:
  0.0 103.4 jit_solution(8420361447536012116)
XLA Ops:
  0.6 2.4 %prepare_keys.1 = (bf16[384,256]{1,0:T(8,128)(2,1)}, bf16[384,256]{1,0:T(8,128)(2,1)}, bf16[384,256]{1,0:T(8,128)(2,1)}, bf16[2,384,256]{2,1,0:T(8,128)(2,1)}, f32[8,128]{1,0:T(8,128)}) custom-call(bf16[128,512]{1,0:T(8,128)(2,1)} %pk.1, bf16[128,512]{1,0:T(8,128)(2,1)} %pv.1, bf16[256,512]{1,0:T(8,128)(2,1)} %bitcast.15, bf16[256,512]{1,0:T(8,128)(2,1)} %bitcast.16), custom_call_target="tpu_custom_call" | custom-call | tf_op jit(solution)/shard_map/prepare_keys/pallas_call | solution.py:553
  3.6 2.6 %collective-permute-start.4 = (bf16[384,256]{1,0:T(8,128)(2,1)}, bf16[384,256]{1,0:T(8,128)(2,1)S(1)}, u32[]{:S(2)}, u32[]{:S(2)}) collective-permute-start(bf16[384,256]{1,0:T(8,128)(2,1)} %get-tuple-element.88), channel_id=1, source_target_pairs={{0,20},{4,16},{8,28},{12,24},{16,4},{20,0},{24,12},{28,8},{1,21},{... | collective-permute-start | bytes 589832 | tf_op jit(solution)/shard_map/ppermute | solution.py:547
  6.2 1.2 %collective-permute-start.2 = (bf16[384,256]{1,0:T(8,128)(2,1)}, bf16[384,256]{1,0:T(8,128)(2,1)S(1)}, u32[]{:S(2)}, u32[]{:S(2)}) collective-permute-start(bf16[384,256]{1,0:T(8,128)(2,1)} %get-tuple-element.88), channel_id=1, source_target_pairs={{0,12},{4,8},{8,4},{12,0},{16,28},{20,24},{24,20},{28,16},{1,13},{... | collective-permute-start | bytes 589832 | tf_op jit(solution)/shard_map/ppermute | solution.py:547
  8.3 0.7 pad_add_fusion.place
  8.9 6.5 %prepare_rows.1 = (bf16[2,288,1408]{2,1,0:T(8,128)(2,1)}, bf16[288,1408]{1,0:T(8,128)(2,1)}, bf16[288,1408]{1,0:T(8,128)(2,1)}) custom-call(s32[3]{0:T(128)} %pad_add_fusion.place, f32[8,128]{1,0:T(8,128)} %get-tuple-element.89.token, bf16[32,2560]{1,0:T(8,128)(2,1)} %pq.1, bf16[32,2560]{1,0:T(8,128)(2,1)} %po.1, bf16[32,2560]{1,0:T(8,128)(2,1)} %pg.1, ...), custom_call_target="tpu_custom_call" | custom-call | flops 1006632960 | bytes 13107200 | tf_op jit(solution)/shard_map/prepare_rows/pallas_call | solution.py:553
  15.4 0.7 collective-permute-done.3.refs_6_
  16.1 1.8 %collective-permute-done.1.refs_4_ = bf16[384,256]{1,0:T(8,128)(2,1)S(1)} collective-permute-done((bf16[384,256]{1,0:T(8,128)(2,1)}, bf16[384,256]{1,0:T(8,128)(2,1)S(1)}, u32[]{:S(2)}, u32[]{:S(2)}) %collective-permute-start.1) | collective-permute-done | bytes 196640 | tf_op jit(solution)/shard_map/ppermute | solution.py:547
  17.9 1.9 %collective-permute-start.7 = (bf16[384,256]{1,0:T(8,128)(2,1)S(1)}, bf16[384,256]{1,0:T(8,128)(2,1)S(1)}, u32[]{:S(2)}, u32[]{:S(2)}) collective-permute-start(bf16[384,256]{1,0:T(8,128)(2,1)S(1)} %collective-permute-done.4.refs_7_), channel_id=1, source_target_pairs={{0,8},{4,12},{8,0},{12,4},{16,24},{20,28},{24,16},{28,20},{1,9},{5... | collective-permute-start | bytes 589832 | tf_op jit(solution)/shard_map/ppermute | solution.py:547
  19.9 1.7 %collective-permute-done.5.refs_1_ = bf16[2,288,1408]{2,1,0:T(8,128)(2,1)S(1)} collective-permute-done((bf16[2,288,1408]{2,1,0:T(8,128)(2,1)}, bf16[2,288,1408]{2,1,0:T(8,128)(2,1)S(1)}, u32[]{:S(2)}, u32[]{:S(2)}) %collective-permute-start.5) | collective-permute-done | bytes 1622048 | tf_op jit(solution)/shard_map/ppermute | solution.py:547
  21.6 1.5 %collective-permute-start.14 = (bf16[2,384,256]{2,1,0:T(8,128)(2,1)S(1)}, bf16[2,384,256]{2,1,0:T(8,128)(2,1)S(1)}, u32[]{:S(2)}, u32[]{:S(2)}) collective-permute-start(bf16[2,384,256]{2,1,0:T(8,128)(2,1)S(1)} %pad_maximum_fusion.refs_2_), channel_id=1, source_target_pairs={{0,24},{4,28},{8,16},{12,20},{16,8},{20,12},{24,0},{28,4},{1,25},{... | collective-permute-start | bytes 1179656 | tf_op jit(solution)/shard_map/ppermute | solution.py:547
  23.1 1.5 %collective-permute-start.13 = (bf16[2,384,256]{2,1,0:T(8,128)(2,1)S(1)}, bf16[2,384,256]{2,1,0:T(8,128)(2,1)S(1)}, u32[]{:S(2)}, u32[]{:S(2)}) collective-permute-start(bf16[2,384,256]{2,1,0:T(8,128)(2,1)S(1)} %pad_maximum_fusion.refs_2_), channel_id=1, source_target_pairs={{0,16},{4,20},{8,24},{12,28},{16,0},{20,4},{24,8},{28,12},{1,17},{... | collective-permute-start | bytes 1179656 | tf_op jit(solution)/shard_map/ppermute | solution.py:547
  25.7 1.1 %copy-done.2 = bf16[288,1408]{1,0:T(8,128)(2,1)S(1)} copy-done((bf16[288,1408]{1,0:T(8,128)(2,1)S(1)}, bf16[288,1408]{1,0:T(8,128)(2,1)}, u32[]{:S(2)}) %copy-start.2) | copy-done | bytes 811032
  26.8 16.9 %attend.2 = (bf16[288,640]{1,0:T(8,128)(2,1)S(1)}, bf16[288,640]{1,0:T(8,128)(2,1)S(1)}, bf16[2,384,256]{2,1,0:T(8,128)(2,1)S(1)}, bf16[2,384,256]{2,1,0:T(8,128...) custom-call(s32[3]{0:T(128)S(1)} %copy-done, s32[8]{0:T(128)S(1)} %copy-done.4, ...), custom_call_target="tpu_custom_call" | custom-call | flops 6710886400 | bytes 8388608 | tf_op jit(solution)/shard_map/attend/pallas_call | solution.py:553
  43.8 4.0 %collective-permute-start.8 = (bf16[2,384,256]{2,1,0:T(8,128)(2,1)S(1)}, bf16[2,384,256]{2,1,0:T(8,128)(2,1)S(1)}, u32[]{:S(2)}, u32[]{:S(2)}) collective-permute-start(bf16[2,384,256]{2,1,0:T(8,128)(2,1)S(1)} %get-tuple-element.105), channel_id=1, source_target_pairs={{0,8},{4,12},{8,0},{12,4},{16,24},{20,28},{24,16},{28,20},{1,9},{5... | collective-permute-start | bytes 1179656 | tf_op jit(solution)/shard_map/ppermute | solution.py:547
  47.8 3.4 %collective-permute-start.9 = (bf16[2,384,256]{2,1,0:T(8,128)(2,1)S(1)}, bf16[2,384,256]{2,1,0:T(8,128)(2,1)S(1)}, u32[]{:S(2)}, u32[]{:S(2)}) collective-permute-start(bf16[2,384,256]{2,1,0:T(8,128)(2,1)S(1)} %get-tuple-element.106), channel_id=1, source_target_pairs={{0,16},{4,20},{8,24},{12,28},{16,0},{20,4},{24,8},{28,12},{1,17},{... | collective-permute-start | bytes 1179656 | tf_op jit(solution)/shard_map/ppermute | solution.py:547
  51.2 1.4 %collective-permute-start.10 = (bf16[2,384,256]{2,1,0:T(8,128)(2,1)S(1)}, bf16[2,384,256]{2,1,0:T(8,128)(2,1)S(1)}, u32[]{:S(2)}, u32[]{:S(2)}) collective-permute-start(bf16[2,384,256]{2,1,0:T(8,128)(2,1)S(1)} %get-tuple-element.107), channel_id=1, source_target_pairs={{0,24},{4,28},{8,16},{12,20},{16,8},{20,12},{24,0},{28,4},{1,25},{... | collective-permute-start | bytes 1179656 | tf_op jit(solution)/shard_map/ppermute | solution.py:547
  52.7 16.8 %attend.3 = (bf16[288,640]{1,0:T(8,128)(2,1)S(1)}, bf16[288,640]{1,0:T(8,128)(2,1)S(1)}, bf16[2,256,256]{2,1,0:T(8,128)(2,1)S(1)}, bf16[2,256,256]{2,1,0:T(8,128...) custom-call(s32[3]{0:T(128)S(1)} %copy-done, ...), custom_call_target="tpu_custom_call" | custom-call | flops 6710886400 | bytes 8388608 | tf_op jit(solution)/shard_map/attend/pallas_call | solution.py:553
  69.5 1.0 collective-permute-done.10.refs_3_
  70.5 1.7 %collective-permute-start.15 = (bf16[2,128,256]{2,1,0:T(8,128)(2,1)S(1)}, bf16[2,128,256]{2,1,0:T(8,128)(2,1)S(1)}, u32[]{:S(2)}, u32[]{:S(2)}) collective-permute-start(bf16[2,128,256]{2,1,0:T(8,128)(2,1)S(1)} %get-tuple-element.125), channel_id=1, source_target_pairs={{0,8},{4,12},{8,0},{12,4},{16,24},{20,28},{24,16},{28,20},{1,9},{5... | collective-permute-start | bytes 393224 | tf_op jit(solution)/shard_map/ppermute | solution.py:547
  72.2 4.8 %collective-permute-start.16 = (bf16[2,128,256]{2,1,0:T(8,128)(2,1)S(1)}, bf16[2,128,256]{2,1,0:T(8,128)(2,1)S(1)}, u32[]{:S(2)}, u32[]{:S(2)}) collective-permute-start(bf16[2,128,256]{2,1,0:T(8,128)(2,1)S(1)} %get-tuple-element.126), channel_id=1, source_target_pairs={{0,16},{4,20},{8,24},{12,28},{16,0},{20,4},{24,8},{28,12},{1,17},{... | collective-permute-start | bytes 393224 | tf_op jit(solution)/shard_map/ppermute | solution.py:547
  77.0 1.4 %collective-permute-start.17 = (bf16[2,128,256]{2,1,0:T(8,128)(2,1)S(1)}, bf16[2,128,256]{2,1,0:T(8,128)(2,1)S(1)}, u32[]{:S(2)}, u32[]{:S(2)}) collective-permute-start(bf16[2,128,256]{2,1,0:T(8,128)(2,1)S(1)} %get-tuple-element.127), channel_id=1, source_target_pairs={{0,24},{4,28},{8,16},{12,20},{16,8},{20,12},{24,0},{28,4},{1,25},{... | collective-permute-start | bytes 393224 | tf_op jit(solution)/shard_map/ppermute | solution.py:547
  78.4 4.7 %collective-permute-done.16.refs_6_ = bf16[2,128,256]{2,1,0:T(8,128)(2,1)S(1)} collective-permute-done((bf16[2,128,256]{2,1,0:T(8,128)(2,1)S(1)}, bf16[2,128,256]{2,1,0:T(8,128)(2,1)S(1)}, u32[]{:S(2)}, u32[]{:S(2)}) %collective-permute-start.16) | collective-permute-done | bytes 131104 | tf_op jit(solution)/shard_map/ppermute | solution.py:547
  83.1 1.9 %collective-permute-done.17.refs_7_ = bf16[2,128,256]{2,1,0:T(8,128)(2,1)S(1)} collective-permute-done((bf16[2,128,256]{2,1,0:T(8,128)(2,1)S(1)}, bf16[2,128,256]{2,1,0:T(8,128)(2,1)S(1)}, u32[]{:S(2)}, u32[]{:S(2)}) %collective-permute-start.17) | collective-permute-done | bytes 131104 | tf_op jit(solution)/shard_map/ppermute | solution.py:547
  85.0 0.6 collective-permute-start.22
  85.6 1.7 %collective-permute-start.23 = (bf16[2,256,256]{2,1,0:T(8,128)(2,1)S(1)}, bf16[2,256,256]{2,1,0:T(8,128)(2,1)S(1)}, u32[]{:S(2)}, u32[]{:S(2)}) collective-permute-start(bf16[2,256,256]{2,1,0:T(8,128)(2,1)S(1)} %get-tuple-element.151), channel_id=1, source_target_pairs={{0,16},{4,20},{8,24},{12,28},{16,0},{20,4},{24,8},{28,12},{1,17},{... | collective-permute-start | bytes 786440 | tf_op jit(solution)/shard_map/ppermute | solution.py:547
  87.3 1.2 %collective-permute-start.24 = (bf16[2,256,256]{2,1,0:T(8,128)(2,1)S(1)}, bf16[2,256,256]{2,1,0:T(8,128)(2,1)S(1)}, u32[]{:S(2)}, u32[]{:S(2)}) collective-permute-start(bf16[2,256,256]{2,1,0:T(8,128)(2,1)S(1)} %get-tuple-element.152), channel_id=1, source_target_pairs={{0,24},{4,28},{8,16},{12,20},{16,8},{20,12},{24,0},{28,4},{1,25},{... | collective-permute-start | bytes 786440 | tf_op jit(solution)/shard_map/ppermute | solution.py:547
  88.5 0.9 collect_first.1
  89.5 6.1 %collective-permute-done.19.refs_5_ = bf16[4,32,256]{2,1,0:T(8,128)(2,1)S(1)} collective-permute-done((bf16[4,32,256]{2,1,0:T(8,128)(2,1)S(1)}, bf16[4,32,256]{2,1,0:T(8,128)(2,1)S(1)}, u32[]{:S(2)}, u32[]{:S(2)}) %collective-permute-start.19) | collective-permute-done | bytes 65568 | tf_op jit(solution)/shard_map/ppermute | solution.py:705
  95.6 2.2 %finish_queries.1 = (bf16[32,2560]{1,0:T(8,128)(2,1)}, bf16[256,2560]{1,0:T(8,128)(2,1)}) custom-call(s32[3]{0:T(128)S(1)} %copy-done, bf16[288,640]{1,0:T(8,128)(2,1)S(1)} %get-tuple-element.141.refs_0_, bf16[288,640]{1,0:T(8,128)(2,1)S(1)} %collective-permute-done.11.refs_1_, bf16[288,640]{1,0:T(8,128)(2,1)S(1)} %get-tuple-element.143.refs_2_, ...), custom_call_target="tpu_custom_call" | custom-call | flops 335544320 | bytes 5242880 | tf_op jit(solution)/shard_map/finish_queries/pallas_call | solution.py:553
  97.8 2.1 %collective-permute-done.21.refs_7_ = bf16[4,32,256]{2,1,0:T(8,128)(2,1)S(1)} collective-permute-done((bf16[4,32,256]{2,1,0:T(8,128)(2,1)S(1)}, bf16[4,32,256]{2,1,0:T(8,128)(2,1)S(1)}, u32[]{:S(2)}, u32[]{:S(2)}) %collective-permute-start.21) | collective-permute-done | bytes 65568 | tf_op jit(solution)/shard_map/ppermute | solution.py:705
  100.1 1.6 %collective-permute-done.25.theirs = bf16[576,256]{1,0:T(8,128)(2,1)S(1)} collective-permute-done((bf16[576,256]{1,0:T(8,128)(2,1)S(1)}, bf16[576,256]{1,0:T(8,128)(2,1)S(1)}, u32[]{:S(2)}, u32[]{:S(2)}) %collective-permute-start.25) | collective-permute-done | bytes 294944 | tf_op jit(solution)/shard_map/ppermute | solution.py:547
  101.7 1.7 %finish_keys.1 = (bf16[32,512]{1,0:T(8,128)(2,1)}, bf16[32,512]{1,0:T(8,128)(2,1)}, bf16[256,512]{1,0:T(8,128)(2,1)}, bf16[256,512]{1,0:T(8,128)(2,1)}) custom-call(s32[3]{0:T(128)S(1)} %copy-done, f32[256,256]{1,0:T(8,128)S(1)} %get-tuple-element.148.reply0, f32[256,256]{1,0:T(8,128)S(1)} %get-tuple-element.158.reply1, ...), custom_call_target="tpu_custom_call" | custom-call | tf_op jit(solution)/shard_map/finish_keys/pallas_call | solution.py:553
  (45 shorter events, 3.0 us)
Async XLA Ops:
  3.1 14.8 %collective-permute-start = (bf16[2,384,256]{2,1,0:T(8,128)(2,1)}, bf16[2,384,256]{2,1,0:T(8,128)(2,1)S(1)}, u32[]{:S(2)}, u32[]{:S(2)}) collective-permute-start(bf16[2,384,256]{2,1,0:T(8,128)(2,1)} %get-tuple-element.87), channel_id=1, source_target_pairs={{0,4},{4,0},{8,12},{12,8},{16,20},{20,16},{24,28},{28,24},{1,5},{5... | collective-permute-start | bytes 1179656 | tf_op jit(solution)/shard_map/ppermute | solution.py:547
  3.6 11.8 %collective-permute-start.4 = (bf16[384,256]{1,0:T(8,128)(2,1)}, bf16[384,256]{1,0:T(8,128)(2,1)S(1)}, u32[]{:S(2)}, u32[]{:S(2)}) collective-permute-start(bf16[384,256]{1,0:T(8,128)(2,1)} %get-tuple-element.88), channel_id=1, source_target_pairs={{0,20},{4,16},{8,28},{12,24},{16,4},{20,0},{24,12},{28,8},{1,21},{... | collective-permute-start | bytes 589832 | tf_op jit(solution)/shard_map/ppermute | solution.py:547
  6.2 9.2 %collective-permute-start.2 = (bf16[384,256]{1,0:T(8,128)(2,1)}, bf16[384,256]{1,0:T(8,128)(2,1)S(1)}, u32[]{:S(2)}, u32[]{:S(2)}) collective-permute-start(bf16[384,256]{1,0:T(8,128)(2,1)} %get-tuple-element.88), channel_id=1, source_target_pairs={{0,12},{4,8},{8,4},{12,0},{16,28},{20,24},{24,20},{28,16},{1,13},{... | collective-permute-start | bytes 589832 | tf_op jit(solution)/shard_map/ppermute | solution.py:547
  7.4 8.7 %collective-permute-start.3 = (bf16[384,256]{1,0:T(8,128)(2,1)}, bf16[384,256]{1,0:T(8,128)(2,1)S(1)}, u32[]{:S(2)}, u32[]{:S(2)}) collective-permute-start(bf16[384,256]{1,0:T(8,128)(2,1)} %get-tuple-element.98.refs_2_), channel_id=1, source_target_pairs={{0,16},{4,20},{8,24},{12,28},{16,0},{20,4},{24,8},{28,12},{1,17},{... | collective-permute-start | bytes 589832 | tf_op jit(solution)/shard_map/ppermute | solution.py:547
  7.9 9.9 %collective-permute-start.1 = (bf16[384,256]{1,0:T(8,128)(2,1)}, bf16[384,256]{1,0:T(8,128)(2,1)S(1)}, u32[]{:S(2)}, u32[]{:S(2)}) collective-permute-start(bf16[384,256]{1,0:T(8,128)(2,1)} %get-tuple-element.98.refs_2_), channel_id=1, source_target_pairs={{0,8},{4,12},{8,0},{12,4},{16,24},{20,28},{24,16},{28,20},{1,9},{5... | collective-permute-start | bytes 589832 | tf_op jit(solution)/shard_map/ppermute | solution.py:547
  8.9 12.7 %copy-start.6 = (bf16[384,256]{1,0:T(8,128)(2,1)S(1)}, bf16[384,256]{1,0:T(8,128)(2,1)}, u32[]{:S(2)}) copy-start(bf16[384,256]{1,0:T(8,128)(2,1)} %get-tuple-element.110) | copy-start | bytes 589828
  8.9 16.7 %copy-start = (s32[3]{0:T(128)S(1)}, s32[3]{0:T(128)}, u32[]{:S(2)}) copy-start(s32[3]{0:T(128)} %pad_add_fusion.place) | copy-start | bytes 40
  8.9 16.7 %copy-start.3 = (bf16[384,256]{1,0:T(8,128)(2,1)S(1)}, bf16[384,256]{1,0:T(8,128)(2,1)}, u32[]{:S(2)}) copy-start(bf16[384,256]{1,0:T(8,128)(2,1)} %get-tuple-element.98.refs_2_) | copy-start | bytes 589828
  8.9 16.7 %copy-start.4 = (s32[8]{0:T(128)S(1)}, s32[8]{0:T(128)}, u32[]{:S(2)}) copy-start(s32[8]{0:T(128)} %reply_len.3) | copy-start | bytes 100
  8.9 16.7 %copy-start.5 = (s32[8]{0:T(128)S(1)}, s32[8]{0:T(128)}, u32[]{:S(2)}) copy-start(s32[8]{0:T(128)} %reply_slot.3) | copy-start | bytes 100
  17.9 3.7 %collective-permute-start.5 = (bf16[2,288,1408]{2,1,0:T(8,128)(2,1)}, bf16[2,288,1408]{2,1,0:T(8,128)(2,1)S(1)}, u32[]{:S(2)}, u32[]{:S(2)}) collective-permute-start(bf16[2,288,1408]{2,1,0:T(8,128)(2,1)} %get-tuple-element.95), channel_id=1, source_target_pairs={{0,4},{4,0},{8,12},{12,8},{16,20},{20,16},{24,28},{28,24},{1,5},{5... | collective-permute-start | bytes 4866056 | tf_op jit(solution)/shard_map/ppermute | solution.py:547
  17.9 7.3 %collective-permute-start.6 = (bf16[384,256]{1,0:T(8,128)(2,1)S(1)}, bf16[384,256]{1,0:T(8,128)(2,1)S(1)}, u32[]{:S(2)}, u32[]{:S(2)}) collective-permute-start(bf16[384,256]{1,0:T(8,128)(2,1)S(1)} %collective-permute-done.1.refs_4_), channel_id=1, source_target_pairs={{0,16},{4,20},{8,24},{12,28},{16,0},{20,4},{24,8},{28,12},{1,17},{... | collective-permute-start | bytes 589832 | tf_op jit(solution)/shard_map/ppermute | solution.py:547
  17.9 7.7 %collective-permute-start.7 = (bf16[384,256]{1,0:T(8,128)(2,1)S(1)}, bf16[384,256]{1,0:T(8,128)(2,1)S(1)}, u32[]{:S(2)}, u32[]{:S(2)}) collective-permute-start(bf16[384,256]{1,0:T(8,128)(2,1)S(1)} %collective-permute-done.4.refs_7_), channel_id=1, source_target_pairs={{0,8},{4,12},{8,0},{12,4},{16,24},{20,28},{24,16},{28,20},{1,9},{5... | collective-permute-start | bytes 589832 | tf_op jit(solution)/shard_map/ppermute | solution.py:547
  21.6 31.1 %copy-start.1 = (bf16[288,1408]{1,0:T(8,128)(2,1)S(1)}, bf16[288,1408]{1,0:T(8,128)(2,1)}, u32[]{:S(2)}) copy-start(bf16[288,1408]{1,0:T(8,128)(2,1)} %get-tuple-element.109.refs_0_) | copy-start | bytes 2433028
  21.6 26.2 %collective-permute-start.14 = (bf16[2,384,256]{2,1,0:T(8,128)(2,1)S(1)}, bf16[2,384,256]{2,1,0:T(8,128)(2,1)S(1)}, u32[]{:S(2)}, u32[]{:S(2)}) collective-permute-start(bf16[2,384,256]{2,1,0:T(8,128)(2,1)S(1)} %pad_maximum_fusion.refs_2_), channel_id=1, source_target_pairs={{0,24},{4,28},{8,16},{12,20},{16,8},{20,12},{24,0},{28,4},{1,25},{... | collective-permute-start | bytes 1179656 | tf_op jit(solution)/shard_map/ppermute | solution.py:547
  23.1 28.1 %collective-permute-start.13 = (bf16[2,384,256]{2,1,0:T(8,128)(2,1)S(1)}, bf16[2,384,256]{2,1,0:T(8,128)(2,1)S(1)}, u32[]{:S(2)}, u32[]{:S(2)}) collective-permute-start(bf16[2,384,256]{2,1,0:T(8,128)(2,1)S(1)} %pad_maximum_fusion.refs_2_), channel_id=1, source_target_pairs={{0,16},{4,20},{8,24},{12,28},{16,0},{20,4},{24,8},{28,12},{1,17},{... | collective-permute-start | bytes 1179656 | tf_op jit(solution)/shard_map/ppermute | solution.py:547
  24.6 28.0 %collective-permute-start.12 = (bf16[2,384,256]{2,1,0:T(8,128)(2,1)S(1)}, bf16[2,384,256]{2,1,0:T(8,128)(2,1)S(1)}, u32[]{:S(2)}, u32[]{:S(2)}) collective-permute-start(bf16[2,384,256]{2,1,0:T(8,128)(2,1)S(1)} %pad_maximum_fusion.refs_2_), channel_id=1, source_target_pairs={{0,8},{4,12},{8,0},{12,4},{16,24},{20,28},{24,16},{28,20},{1,9},{5... | collective-permute-start | bytes 1179656 | tf_op jit(solution)/shard_map/ppermute | solution.py:547
  43.7 25.7 %collective-permute-start.11 = (bf16[288,640]{1,0:T(8,128)(2,1)S(1)}, bf16[288,640]{1,0:T(8,128)(2,1)S(1)}, u32[]{:S(2)}, u32[]{:S(2)}) collective-permute-start(bf16[288,640]{1,0:T(8,128)(2,1)S(1)} %get-tuple-element.108), channel_id=1, source_target_pairs={{0,4},{4,0},{8,12},{12,8},{16,20},{20,16},{24,28},{28,24},{1,5},{5... | collective-permute-start | bytes 1105928 | tf_op jit(solution)/shard_map/ppermute | solution.py:547
  43.8 25.7 %collective-permute-start.8 = (bf16[2,384,256]{2,1,0:T(8,128)(2,1)S(1)}, bf16[2,384,256]{2,1,0:T(8,128)(2,1)S(1)}, u32[]{:S(2)}, u32[]{:S(2)}) collective-permute-start(bf16[2,384,256]{2,1,0:T(8,128)(2,1)S(1)} %get-tuple-element.105), channel_id=1, source_target_pairs={{0,8},{4,12},{8,0},{12,4},{16,24},{20,28},{24,16},{28,20},{1,9},{5... | collective-permute-start | bytes 1179656 | tf_op jit(solution)/shard_map/ppermute | solution.py:547
  47.8 21.7 %collective-permute-start.9 = (bf16[2,384,256]{2,1,0:T(8,128)(2,1)S(1)}, bf16[2,384,256]{2,1,0:T(8,128)(2,1)S(1)}, u32[]{:S(2)}, u32[]{:S(2)}) collective-permute-start(bf16[2,384,256]{2,1,0:T(8,128)(2,1)S(1)} %get-tuple-element.106), channel_id=1, source_target_pairs={{0,16},{4,20},{8,24},{12,28},{16,0},{20,4},{24,8},{28,12},{1,17},{... | collective-permute-start | bytes 1179656 | tf_op jit(solution)/shard_map/ppermute | solution.py:547
  51.2 19.2 %collective-permute-start.10 = (bf16[2,384,256]{2,1,0:T(8,128)(2,1)S(1)}, bf16[2,384,256]{2,1,0:T(8,128)(2,1)S(1)}, u32[]{:S(2)}, u32[]{:S(2)}) collective-permute-start(bf16[2,384,256]{2,1,0:T(8,128)(2,1)S(1)} %get-tuple-element.107), channel_id=1, source_target_pairs={{0,24},{4,28},{8,16},{12,20},{16,8},{20,12},{24,0},{28,4},{1,25},{... | collective-permute-start | bytes 1179656 | tf_op jit(solution)/shard_map/ppermute | solution.py:547
  70.5 14.5 %collective-permute-start.18 = (bf16[288,640]{1,0:T(8,128)(2,1)S(1)}, bf16[288,640]{1,0:T(8,128)(2,1)S(1)}, u32[]{:S(2)}, u32[]{:S(2)}) collective-permute-start(bf16[288,640]{1,0:T(8,128)(2,1)S(1)} %get-tuple-element.128), channel_id=1, source_target_pairs={{0,4},{4,0},{8,12},{12,8},{16,20},{20,16},{24,28},{28,24},{1,5},{5... | collective-permute-start | bytes 1105928 | tf_op jit(solution)/shard_map/ppermute | solution.py:547
  70.5 7.9 %collective-permute-start.15 = (bf16[2,128,256]{2,1,0:T(8,128)(2,1)S(1)}, bf16[2,128,256]{2,1,0:T(8,128)(2,1)S(1)}, u32[]{:S(2)}, u32[]{:S(2)}) collective-permute-start(bf16[2,128,256]{2,1,0:T(8,128)(2,1)S(1)} %get-tuple-element.125), channel_id=1, source_target_pairs={{0,8},{4,12},{8,0},{12,4},{16,24},{20,28},{24,16},{28,20},{1,9},{5... | collective-permute-start | bytes 393224 | tf_op jit(solution)/shard_map/ppermute | solution.py:547
  72.2 10.9 %collective-permute-start.16 = (bf16[2,128,256]{2,1,0:T(8,128)(2,1)S(1)}, bf16[2,128,256]{2,1,0:T(8,128)(2,1)S(1)}, u32[]{:S(2)}, u32[]{:S(2)}) collective-permute-start(bf16[2,128,256]{2,1,0:T(8,128)(2,1)S(1)} %get-tuple-element.126), channel_id=1, source_target_pairs={{0,16},{4,20},{8,24},{12,28},{16,0},{20,4},{24,8},{28,12},{1,17},{... | collective-permute-start | bytes 393224 | tf_op jit(solution)/shard_map/ppermute | solution.py:547
  77.0 8.0 %collective-permute-start.17 = (bf16[2,128,256]{2,1,0:T(8,128)(2,1)S(1)}, bf16[2,128,256]{2,1,0:T(8,128)(2,1)S(1)}, u32[]{:S(2)}, u32[]{:S(2)}) collective-permute-start(bf16[2,128,256]{2,1,0:T(8,128)(2,1)S(1)} %get-tuple-element.127), channel_id=1, source_target_pairs={{0,24},{4,28},{8,16},{12,20},{16,8},{20,12},{24,0},{28,4},{1,25},{... | collective-permute-start | bytes 393224 | tf_op jit(solution)/shard_map/ppermute | solution.py:547
  85.0 14.9 %collective-permute-start.22 = (bf16[2,256,256]{2,1,0:T(8,128)(2,1)S(1)}, bf16[2,256,256]{2,1,0:T(8,128)(2,1)S(1)}, u32[]{:S(2)}, u32[]{:S(2)}) collective-permute-start(bf16[2,256,256]{2,1,0:T(8,128)(2,1)S(1)} %get-tuple-element.150), channel_id=1, source_target_pairs={{0,8},{4,12},{8,0},{12,4},{16,24},{20,28},{24,16},{28,20},{1,9},{5... | collective-permute-start | bytes 786440 | tf_op jit(solution)/shard_map/ppermute | solution.py:547
  85.6 14.3 %collective-permute-start.23 = (bf16[2,256,256]{2,1,0:T(8,128)(2,1)S(1)}, bf16[2,256,256]{2,1,0:T(8,128)(2,1)S(1)}, u32[]{:S(2)}, u32[]{:S(2)}) collective-permute-start(bf16[2,256,256]{2,1,0:T(8,128)(2,1)S(1)} %get-tuple-element.151), channel_id=1, source_target_pairs={{0,16},{4,20},{8,24},{12,28},{16,0},{20,4},{24,8},{28,12},{1,17},{... | collective-permute-start | bytes 786440 | tf_op jit(solution)/shard_map/ppermute | solution.py:547
  87.3 12.6 %collective-permute-start.24 = (bf16[2,256,256]{2,1,0:T(8,128)(2,1)S(1)}, bf16[2,256,256]{2,1,0:T(8,128)(2,1)S(1)}, u32[]{:S(2)}, u32[]{:S(2)}) collective-permute-start(bf16[2,256,256]{2,1,0:T(8,128)(2,1)S(1)} %get-tuple-element.152), channel_id=1, source_target_pairs={{0,24},{4,28},{8,16},{12,20},{16,8},{20,12},{24,0},{28,4},{1,25},{... | collective-permute-start | bytes 786440 | tf_op jit(solution)/shard_map/ppermute | solution.py:547
  89.4 6.2 %collective-permute-start.19 = (bf16[4,32,256]{2,1,0:T(8,128)(2,1)S(1)}, bf16[4,32,256]{2,1,0:T(8,128)(2,1)S(1)}, u32[]{:S(2)}, u32[]{:S(2)}) collective-permute-start(bf16[4,32,256]{2,1,0:T(8,128)(2,1)S(1)} %get-tuple-element.138), channel_id=1, source_target_pairs={{0,1},{1,2},{2,3},{3,0},{4,5},{5,6},{6,7},{7,4},{8,9},{9,10},{10,1... | collective-permute-start | bytes 196616 | tf_op jit(solution)/shard_map/ppermute | solution.py:705
  89.4 8.3 %collective-permute-start.20 = (bf16[4,32,256]{2,1,0:T(8,128)(2,1)S(1)}, bf16[4,32,256]{2,1,0:T(8,128)(2,1)S(1)}, u32[]{:S(2)}, u32[]{:S(2)}) collective-permute-start(bf16[4,32,256]{2,1,0:T(8,128)(2,1)S(1)} %get-tuple-element.139), channel_id=1, source_target_pairs={{0,2},{1,3},{2,0},{3,1},{4,6},{5,7},{6,4},{7,5},{8,10},{9,11},{10,... | collective-permute-start | bytes 196616 | tf_op jit(solution)/shard_map/ppermute | solution.py:705
  95.6 4.3 %collective-permute-start.21 = (bf16[4,32,256]{2,1,0:T(8,128)(2,1)S(1)}, bf16[4,32,256]{2,1,0:T(8,128)(2,1)S(1)}, u32[]{:S(2)}, u32[]{:S(2)}) collective-permute-start(bf16[4,32,256]{2,1,0:T(8,128)(2,1)S(1)} %get-tuple-element.140), channel_id=1, source_target_pairs={{0,3},{1,0},{2,1},{3,2},{4,7},{5,4},{6,5},{7,6},{8,11},{9,8},{10,9... | collective-permute-start | bytes 196616 | tf_op jit(solution)/shard_map/ppermute | solution.py:705
  100.0 1.6 %collective-permute-start.25 = (bf16[576,256]{1,0:T(8,128)(2,1)S(1)}, bf16[576,256]{1,0:T(8,128)(2,1)S(1)}, u32[]{:S(2)}, u32[]{:S(2)}) collective-permute-start(bf16[576,256]{1,0:T(8,128)(2,1)S(1)} %get-tuple-element.160), channel_id=1, source_target_pairs={{0,4},{4,0},{8,12},{12,8},{16,20},{20,16},{24,28},{28,24},{1,5},{5... | collective-permute-start | bytes 884744 | tf_op jit(solution)/shard_map/ppermute | solution.py:547
  (1 other events, 1.1 us)
